TPU v7x, 128 devices: a whole 4x4x4 slice. The times are simulated.
128 devices in a mesh: row: 8 (over x_lo, y), col: 16 (over z, x_hi, core).
Axes of the slice: x: 4 (x_hi: 2, x_lo: 2; x = x_hi * 2 + x_lo), y: 4, z: 4, core: 2. Of those that a mesh axis runs over, the one named last changes fastest.
Arguments:
- activations: bfloat16 [1280, 28672], P('col', 'row'), may hold values from -6 to 6
- gradients: bfloat16 [1280, 8192], P('row', 'col'), may hold values from -0.0014953613 to 0.0014953613
- basis_in: bfloat16 [28672, 28672], P('row', 'col'), may hold values from -0.03125 to 0.03125
- basis_out: bfloat16 [8192, 8192], P('col', 'row'), may hold values from -0.0625 to 0.0625
- eigen_damped: float32 [8192, 28672], P('row', 'col'), may hold values from 0.1 to 4
- pair_ids: int32 [1024], replicated, may hold values from 0 to 3, never falling along the last dimension, each value on 1 to 384 neighbouring positions
Outputs:
- scores: float32 [4, 64], replicated
Inputs may be any that keep to these rules, and one draw needn't show every extreme that they name: `pair_ids`: ids never fall; every pair has 1 to 384 tokens, and some pair has exactly 384.
All inputs are finite; a program needn't handle non-finite values.
Results may differ from a plain program's by a relative error of at most 0.0046.
Values may be sent and summed in bfloat16 or wider, within the bound.
A program may use at most 128 MiB of HBM per device.

v0:
```python
import jax
import jax.numpy as jnp
from jax import lax
from jax.sharding import PartitionSpec as P

PAIRS = 4
QLEN = 4
MOST = 384


def on_device(activations, gradients, basis_in, basis_out, eigen_damped, pair_ids):
    pair_rows = pair_ids.shape[0]
    partial_in = jnp.dot(
        lax.all_gather(activations, "col", axis=0, tiled=True),
        basis_in,
        preferred_element_type=jnp.float32,
    )
    rotated_in = lax.psum(partial_in, "row").astype(jnp.bfloat16)
    partial_out = jnp.dot(
        lax.all_gather(gradients, "row", axis=0, tiled=True),
        basis_out,
        preferred_element_type=jnp.float32,
    )
    rotated_out = lax.psum(partial_out, "col").astype(jnp.bfloat16)
    pair_in = rotated_in[:pair_rows]
    pair_out = rotated_out[:pair_rows]
    query_in = rotated_in[pair_rows:]
    query_out = rotated_out[pair_rows:].astype(jnp.float32)
    labels = jnp.arange(PAIRS, dtype=jnp.int32)
    offsets = jnp.sum((pair_ids[None, :] < labels[:, None]).astype(jnp.int32), axis=1)
    scaled_list = []
    for pair_index in range(PAIRS):
        window_start = offsets[pair_index]
        window_out = lax.dynamic_slice_in_dim(pair_out, window_start, MOST, 0)
        window_in = lax.dynamic_slice_in_dim(pair_in, window_start, MOST, 0)
        window_ids = lax.dynamic_slice_in_dim(pair_ids, window_start, MOST, 0)
        window_out = jnp.where(
            (window_ids == pair_index)[:, None], window_out, jnp.zeros_like(window_out)
        )
        pair_block = lax.dot_general(
            window_out, window_in, (((0,), (0,)), ((), ())), preferred_element_type=jnp.float32
        )
        scaled_list.append((pair_block / eigen_damped).astype(jnp.bfloat16))
    scaled = jnp.stack(scaled_list)
    mapped = jnp.einsum("pif,sf->pis", scaled, query_in, preferred_element_type=jnp.float32)
    per_token = jnp.sum(mapped * query_out.T[None, :, :], axis=1)
    partial_scores = jnp.sum(per_token.reshape(PAIRS, -1, QLEN), axis=2)
    return lax.psum(partial_scores, ("row", "col"))


def solution(mesh):
    return jax.shard_map(
        on_device,
        mesh=mesh,
        in_specs=(
            P("col", "row"),
            P("row", "col"),
            P("row", "col"),
            P("col", "row"),
            P("row", "col"),
            P(),
        ),
        out_specs=P(),
        check_vma=False,
    )
```

profile of v0, /device:TPU:1, one launch (start us, length us, event | category | flops | bytes accessed | tf_op | source)
XLA Modules:
  0.0 509.7 jit_solution(6026030402667832208)
XLA Ops:
  6.5 0.0 copy-start
  6.5 0.0 all-gather.3.cloned.1.call-start
  6.5 0.7 all-gather.3.cloned.1.call-update
  7.3 0.0 all-gather.5.cloned.1.call-start
  7.3 0.7 all-gather.5.cloned.1.call-update
  8.0 0.8 convert_reduce_fusion
  8.8 0.7 fusion.43
  17.0 0.9 dynamic-slice_compare_fusion.3
  18.0 28.9 %all-gather.3.cloned.1.call-done = bf16[1280,512]{1,0:T(8,128)(2,1)} async-done(((bf16[160,512]{1,0:T(8,128)(2,1)}), bf16[1280,512]{1,0:T(8,128)(2,1)}) %all-gather.3.cloned.1.call-update) | async-done | bytes 1310736 | tf_op jit(solution)/shard_map/all_gather | solution.py:20
  46.8 0.0 copy-done
  46.8 5.2 %fusion.44 = f32[1280,1024]{1,0:T(8,128)} fusion(bf16[1280,512]{1,0:T(8,128)(2,1)} %all-gather.3.cloned.1.call-done, bf16[512,1024]{1,0:T(8,128)(2,1)S(1)} %copy-done), kind=kOutput, calls=%fused_computation.55 | convolution fusion | flops 1342177280 | bytes 7602176 | tf_op jit(solution)/shard_map/dot_general | solution.py:19
  52.1 151.5 %all-reduce.3 = bf16[1280,1024]{1,0:T(8,128)(2,1)} all-reduce(f32[1280,1024]{1,0:T(8,128)} %fusion.44), channel_id=1, replica_groups=mesh['row'=8,'col'=16] {'col'}, use_global_device_ids=true, to_apply=%region_1.0 | all-reduce | flops 1310720 | bytes 7864320 | tf_op jit(solution)/shard_map/psum | solution.py:24
  203.6 1.8 slice.32
  205.3 1.1 convert_bitcast_fusion
  206.5 1.3 copy.9
  207.8 0.0 all-gather.5.cloned.1.call-done
  207.8 24.0 %fusion.45 = f32[1280,1792]{1,0:T(8,128)} fusion(bf16[1280,3584]{1,0:T(8,128)(2,1)} %all-gather.5.cloned.1.call-done, bf16[3584,1792]{1,0:T(8,128)(2,1)} %param.8), kind=kOutput, calls=%fused_computation.56 | convolution fusion | flops 16441671680 | bytes 31195136 | tf_op jit(solution)/shard_map/dot_general | solution.py:13
  231.8 179.3 %all-reduce.2 = bf16[1280,1792]{1,0:T(8,128)(2,1)} all-reduce(f32[1280,1792]{1,0:T(8,128)} %fusion.45), channel_id=1, replica_groups=mesh['row'=8,'col'=16] {'row'}, use_global_device_ids=true, to_apply=%region_2.0 | all-reduce | flops 2293760 | bytes 13762560 | tf_op jit(solution)/shard_map/psum | solution.py:18
  411.0 0.0 slice-start
  411.0 2.4 slice.33
  413.5 0.0 slice-start.1
  413.5 5.5 %fusion.11 = bf16[1,1024,1792]{2,1,0:T(8,128)(2,1)S(1)} fusion(f32[1024,1792]{1,0:T(8,128)} %param.10, bf16[1024,1792]{1,0:T(8,128)(2,1)S(1)} %slice.33, s32[]{:T(128)S(6)} %select_n.39, bf16[1024,1024]{1,0:T(8,128)(2,1)S(1)} %slice.32, pred[384]{0:T(512)(128)(4,1)S(1)} %get-tuple-element.7), kind=kOutput, calls=%fused_computation.16 | convolution fusion | flops 1413349376 | bytes 13174272 | tf_op jit(solution)/shard_map/dot_general | solution.py:40
  419.0 0.0 slice-done
  419.0 0.0 slice-done.1
  419.0 2.5 fusion.10
  421.5 2.5 fusion.9
  423.9 0.0 copy-start.2
  424.0 2.5 fusion.8
  426.4 0.0 copy-done.2
  426.4 0.0 copy-start.1
  426.5 6.0 %multiply_reduce_fusion = f32[4,256]{1,0:T(4,128)S(1)} fusion(bf16[1,1024,1792]{2,1,0:T(8,128)(2,1)S(1)} %fusion.11, bf16[1,1024,1792]{2,1,0:T(8,128)(2,1)S(1)} %fusion.10, bf16[1,1024,1792]{2,1,0:T(8,128)(2,1)S(1)} %fusion.9, bf16[1,1024,1792]{2,1,0:T(8,128)(2,1)S(1)} %fusion.8, f32[1024,256]{1,0:T(8,128)S(1)} %copy-done.2, bf16[1280,1792]{1,0:T(8,128)(2,1)} %all-reduce.2), kind=kOutput, calls=%fused_computation.12 | convolution fusion | flops 3782212608 | bytes 16650240 | tf_op jit(solution)/shard_map/pif,sf->pis/dot_general | solution.py:45
  432.4 0.1 reshape.9
  432.6 0.1 reduce_sum.29
  432.7 70.1 %psum.23 = f32[4,64]{1,0:T(4,128)} all-reduce(f32[4,64]{1,0:T(4,128)S(1)} %reduce_sum.29), channel_id=1, replica_groups=mesh['row'=8,'col'=16] {'row','col'}, use_global_device_ids=true, to_apply=%region_5.6 | all-reduce | flops 256 | bytes 2048 | tf_op jit(solution)/shard_map/psum | solution.py:48
  502.8 0.0 copy-done.1
  (1 shorter events, 0.0 us)
Async XLA Ops:
  6.5 40.3 %copy-start = (bf16[512,1024]{1,0:T(8,128)(2,1)S(1)}, bf16[512,1024]{1,0:T(8,128)(2,1)}, u32[]{:S(2)}) copy-start(bf16[512,1024]{1,0:T(8,128)(2,1)} %param.9) | copy-start | bytes 3145732
  6.5 40.3 %all-gather.3.cloned.1.call-start = ((), (), s32[]{:S(2)}) async-start(), calls=%async_computation | async-start | bytes 1474560 | tf_op jit(solution)/shard_map/all_gather | solution.py:20
  7.3 200.5 %all-gather.5.cloned.1.call-start = ((), (), s32[]{:S(2)}) async-start(), calls=%async_computation.1 | async-start | bytes 9748480 | tf_op jit(solution)/shard_map/all_gather | solution.py:14
  411.0 7.9 %slice-start = ((s8[7340032]{0:T(1024)(128)(4,1)}), s8[4194304]{0:T(1024)(128)(4,1)S(1)}, s32[]{:S(2)}) async-start(s8[7340032]{0:T(1024)(128)(4,1)} %bitcast.21), calls=%async_computation.2 | async-start | bytes 8388608
  413.5 5.5 %slice-start.1 = ((s8[7340032]{0:T(1024)(128)(4,1)}), s8[3145728]{0:T(1024)(128)(4,1)S(1)}, s32[]{:S(2)}) async-start(s8[7340032]{0:T(1024)(128)(4,1)} %bitcast.21), calls=%async_computation.3 | async-start | bytes 6291456
  423.9 2.5 copy-start.2
  426.4 76.4 %copy-start.1 = (bf16[512,1024]{1,0:T(8,128)(2,1)S(1)}, bf16[512,1024]{1,0:T(8,128)(2,1)}, u32[]{:S(2)}) copy-start(bf16[512,1024]{1,0:T(8,128)(2,1)} %param.9) | copy-start | bytes 3145732
Sparse Core Ops, SparseCore 0:
  9.0 37.7 all-gather.2
  49.3 114.6 all-gather.4
where the time goes:
time: 510 us
  blocking collectives  401 us (79%)
  matrix products  48.1 us (9%)
  waiting for transfers between devices  30.3 us (6%)
  between operations  21.1 us (4%)
  local copies, waits for them, and re-layouts  6.31 us (1%)
    psum x1, blocking collectives, on_device(): rotated_in = lax.psum(partial_in, 'row').astype(jnp.bfloat16)  179 us
    psum x1, blocking collectives, on_device(): rotated_out = lax.psum(partial_out, 'col').astype(jnp.bfloat16)  152 us
    psum x1, blocking collectives, on_device(): return lax.psum(partial_scores, ('row', 'col'))  70.1 us
    all_gather x1, waiting for transfers between devices, on_device(): lax.all_gather(gradients, 'row', axis=0, tiled=True)  28.9 us
    dot_general x1, matrix products, on_device(): jnp.dot(lax.all_gather(activations, 'col', axis=0, tiled=True), basis_in,...  24 us
    dot_general x4, matrix products, on_device(): lax.dot_general(window_out, window_in, (((0,), (0,)), ((), ())), preferre...  12.9 us
  transfers between devices with their start and end apart: 2, of which 1 were waited for; matrix products, arithmetic and copies ran while one was open for 2% of the time, Pallas kernels for 0%

commit v1 on v0

--- a/solution.py
+++ b/solution.py
@@ -1,27 +1,451 @@
+import functools
+
 import jax
 import jax.numpy as jnp
 from jax import lax
+from jax.experimental import pallas as pl
+from jax.experimental.pallas import tpu as pltpu
 from jax.sharding import PartitionSpec as P
 
 PAIRS = 4
 QLEN = 4
 MOST = 384
+MESH = pl.DeviceIdType.MESH
+BF16 = jnp.bfloat16
+F32 = jnp.float32
+
+
+def aligned(start, multiple, size):
+    return pl.ds(pl.multiple_of(start, multiple), size)
+
+
+class Place:
+    def __init__(self):
+        row, col = lax.axis_index("row"), lax.axis_index("col")
+        self.xlo, self.y = row // 4, lax.rem(row, 4)
+        self.z, self.xhi, self.core = col // 4, lax.rem(col // 2, 2), lax.rem(col, 2)
+
+    def at(self, xlo=None, y=None, z=None, xhi=None, core=None):
+        xlo = self.xlo if xlo is None else xlo
+        y = self.y if y is None else y
+        z = self.z if z is None else z
+        xhi = self.xhi if xhi is None else xhi
+        core = self.core if core is None else core
+        return (xlo * 4 + y, z * 4 + xhi * 2 + core)
+
+
+def remote(src, dst, sends, recvs, number, device):
+    return pltpu.make_async_remote_copy(
+        src_ref=src,
+        dst_ref=dst,
+        send_sem=sends.at[number],
+        recv_sem=recvs.at[number],
+        device_id=device,
+        device_id_type=MESH,
+    )
+
+
+class Gather:
+    def __init__(self, place, buf, slot, sends, recvs, first=None):
+        zp, zm, z2 = (lax.rem(place.z + k, 4) for k in (1, 3, 2))
+        xhi, other = place.xhi, 1 - place.xhi
+        core, twin = place.core, 1 - place.core
+        to_core, to_xhi = place.at(core=twin), place.at(xhi=other)
+        to_zp, to_zm = place.at(z=zp), place.at(z=zm)
+        z = place.z
+        plan = [
+            (z, xhi, to_core), (z, xhi, to_xhi), (z, xhi, to_zp), (z, xhi, to_zm),
+            (z, other, to_core), (z, other, to_zp), (z, other, to_zm),
+            (zm, xhi, to_core), (zm, xhi, to_zp), (zp, xhi, to_core),
+            (zm, other, to_core), (zp, other, to_core), (zp, other, to_zm),
+            (z2, xhi, to_core), (z2, other, to_core),
+        ]
+        self.copies = []
+        for number, (from_z, from_x, device) in enumerate(plan):
+            block = buf.at[slot(from_z, from_x, core)]
+            src = first if number < 4 and first is not None else block
+            self.copies.append(remote(src, block, sends, recvs, number, device))
+
+    def start(self, *numbers):
+        for number in numbers:
+            self.copies[number].start()
+
+    def wait(self, *numbers):
+        for number in numbers:
+            self.copies[number].wait_recv()
+
+    def finish(self):
+        for copy in self.copies:
+            copy.wait_send()
+
+
+def rotate_kernel(
+    act, grad, basis_in, basis_out, rot_in_hbm, rot_out_hbm,
+    a_buf, b_buf, part, send, land, land_x, rot_in,
+    g_buf, bo_buf, part_out, land_core, land_z, land_h, rot_out,
+    a_send, a_recv, d_send, d_recv, e_send, e_recv, f_send, f_recv, u_send, u_recv, local,
+):
+    me = Place()
+    xlo, y, z, xhi, core = me.xlo, me.y, me.z, me.xhi, me.core
+    yp, ym, y2 = (lax.rem(y + k, 4) for k in (1, 3, 2))
+    zp, zm, z2 = (lax.rem(z + k, 4) for k in (1, 3, 2))
+    to_yp, to_ym = me.at(y=yp), me.at(y=ym)
+    to_zp, to_zm = me.at(z=zp), me.at(z=zm)
+    to_xlo, to_xhi, to_core = me.at(xlo=1 - xlo), me.at(xhi=1 - xhi), me.at(core=1 - core)
+    half = 896
+
+    loads = [
+        pltpu.make_async_copy(act, a_buf.at[aligned(80 * (4 * z + 2 * xhi + core), 80, 80)], local.at[0]),
+        pltpu.make_async_copy(grad, g_buf.at[aligned(160 * (4 * xlo + y), 160, 160)], local.at[1]),
+        pltpu.make_async_copy(basis_in, b_buf, local.at[2]),
+        pltpu.make_async_copy(basis_out, bo_buf, local.at[3]),
+    ]
+    for load in loads:
+        load.start()
+
+    barrier = pltpu.get_barrier_semaphore()
+    friends = (to_yp, to_ym, to_zp, to_zm, to_xlo, to_xhi, to_core)
+    for friend in friends:
+        pl.semaphore_signal(barrier, inc=1, device_id=friend, device_id_type=MESH)
+    pl.semaphore_wait(barrier, len(friends))
+
+    gather_a = Gather(
+        me, a_buf, lambda gz, gx, gc: aligned(80 * (4 * gz + 2 * gx + gc), 80, 80), a_send, a_recv, act
+    )
+    gather_a.start(1, 2, 3, 0)
+
+    def g_slot(gy, gx):
+        return aligned(160 * (4 * gx + gy), 160, 160)
+
+    def d_copy(number, rows, device, src=None):
+        block = g_buf.at[rows]
+        return remote(block if src is None else src, block, d_send, d_recv, number, device)
+
+    d = [
+        d_copy(0, g_slot(y, xlo), to_yp, grad),
+        d_copy(1, g_slot(y, xlo), to_ym, grad),
+        d_copy(2, g_slot(y, xlo), to_xlo, grad),
+        d_copy(3, aligned(160 * (4 * xlo + ym), 80, 80), to_yp),
+        d_copy(4, g_slot(ym, xlo), to_xlo),
+        d_copy(5, aligned(160 * (4 * xlo + yp) + 80, 80, 80), to_ym),
+        d_copy(6, g_slot(yp, xlo), to_xlo),
+        d_copy(7, g_slot(y2, xlo), to_xlo),
+    ]
+    d[0].start()
+    d[1].start()
+
+    def gradients_on():
+        d[0].wait_recv()
+        d[3].start()
+        d[1].wait_recv()
+        d[5].start()
+
+    def gradients_across():
+        d[2].start()
+        d[4].start()
+        d[6].start()
+        d[3].wait_recv()
+        d[5].wait_recv()
+        d[7].start()
+
+    own = 640 * core
+
+    def e_rows(ez):
+        return aligned(own + 160 * ez, 160, 160)
+
+    left, right = pl.ds(0, 512), pl.ds(512, 512)
+    e0 = remote(
+        part_out.at[aligned(640 * (1 - core), 640, 640)], land_core, e_send, e_recv, 0, to_core
+    )
+    e = [
+        remote(part_out.at[e_rows(z2), left], land_z.at[0], e_send, e_recv, 1, to_zp),
+        remote(part_out.at[e_rows(z2), right], land_z.at[1], e_send, e_recv, 2, to_zm),
+        remote(part_out.at[e_rows(zm), left], land_z.at[2], e_send, e_recv, 3, to_zm),
+        remote(part_out.at[e_rows(zp), right], land_z.at[3], e_send, e_recv, 4, to_zp),
+        remote(part_out.at[e_rows(zp), left], land_z.at[4], e_send, e_recv, 5, to_zp),
+        remote(part_out.at[e_rows(zm), right], land_z.at[5], e_send, e_recv, 6, to_zm),
+    ]
+    e_x = remote(
+        part_out.at[aligned(own + 160 * z + 80 * (1 - xhi), 80, 80)], land_h, e_send, e_recv, 7, to_xhi
+    )
+    gather_f = Gather(
+        me, rot_out, lambda gz, gx, gc: aligned(640 * gc + 160 * gz + 80 * gx, 80, 80), f_send, f_recv
+    )
+
+    def out_matmul():
+        loads[1].wait()
+        loads[3].wait()
+        d[2].wait_recv()
+        d[4].wait_recv()
+        d[6].wait_recv()
+        d[7].wait_recv()
+
+        @pl.loop(0, 4)
+        def _(n):
+            rows = aligned(320 * n, 320, 320)
+            part_out[rows, :] = jnp.dot(g_buf[rows, :], bo_buf[...], preferred_element_type=F32)
+
+        e0.start()
+
+    def out_core():
+        e0.wait_recv()
+
+        @pl.loop(0, 4)
+        def _(n):
+            rows = aligned(own + 160 * n, 160, 160)
+            part_out[rows, :] += land_core[aligned(160 * n, 160, 160), :]
+
+        for copy in e[:4]:
+            copy.start()
+
+    def out_z():
+        e[0].wait_recv()
+        part_out[e_rows(zp), left] += land_z[0]
+        e[4].start()
+        e[1].wait_recv()
+        part_out[e_rows(zm), right] += land_z[1]
+        e[5].start()
+
+    def out_sum():
+        for copy in e[2:]:
+            copy.wait_recv()
+        part_out[e_rows(z), left] += land_z[4] + land_z[2]
+        part_out[e_rows(z), right] += land_z[5] + land_z[3]
+        e_x.start()
+
+    def out_final():
+        e_x.wait_recv()
+        rows = aligned(own + 160 * z + 80 * xhi, 80, 80)
+        rot_out[rows, :] = (part_out[rows, :] + land_h[...]).astype(BF16)
+        gather_f.start(1, 2, 3, 0)
+
+    unit_z = (z, zm, zp, z2)
+    everything = pl.ds(0, 1792)
+    h0, h1 = pl.ds(0, half), pl.ds(half, half)
+    mine, others = aligned(half * xlo, half, half), aligned(half * (1 - xlo), half, half)
+    units = []
+    for u in range(4):
+        uz = unit_z[u]
+
+        def rows_in_send(oy, uz=uz):
+            return aligned(320 * uz + 80 * oy, 80, 80)
+
+        def from_send(number, oy, cols, device, u=u):
+            return remote(
+                send.at[rows_in_send(oy), cols], land.at[u, number], u_send.at[u], u_recv.at[u], number, device
+            )
+
+        def spread(number, oy, cols, device, u=u):
+            block = rot_in.at[rows_in_send(oy), cols]
+            return remote(block, block, u_send.at[u], u_recv.at[u], number, device)
+
+        units.append(
+            [
+                from_send(0, y2, h0, to_yp),
+                from_send(1, y2, h1, to_ym),
+                from_send(2, ym, h0, to_ym),
+                from_send(3, yp, h1, to_yp),
+                from_send(4, yp, h0, to_yp),
+                from_send(5, ym, h1, to_ym),
+                remote(
+                    send.at[rows_in_send(y), others], land_x.at[u], u_send.at[u], u_recv.at[u], 6, to_xlo
+                ),
+                spread(7, y, mine, to_xlo),
+                spread(8, y, mine, to_yp),
+                spread(9, y, mine, to_ym),
+                spread(10, y, others, to_yp),
+                spread(11, y, others, to_ym),
+                spread(12, ym, mine, to_yp),
+                spread(13, yp, others, to_ym),
+            ]
+        )
+
+    def matmul(u):
+        rows = aligned(320 * unit_z[u], 320, 320)
+
+        @pl.loop(0, 7)
+        def _(n):
+            cols = aligned(256 * n, 256, 256)
+            block = jnp.dot(a_buf[rows, :], b_buf[:, cols], preferred_element_type=F32)
+            part[u % 2, :, cols] = block
+            send[rows, cols] = block.astype(BF16)
+
+        for copy in units[u][:4]:
+            copy.start()
+
+    def part_rows(oy):
+        return aligned(80 * oy, 80, 80)
+
+    def send_rows(u, oy):
+        return aligned(320 * unit_z[u] + 80 * oy, 80, 80)
+
+    def second(u):
+        c = units[u]
+        c[0].wait_recv()
+        send[send_rows(u, yp), h0] = (part[u % 2, part_rows(yp), h0] + land[u, 0].astype(F32)).astype(BF16)
+        c[4].start()
+        c[1].wait_recv()
+        send[send_rows(u, ym), h1] = (part[u % 2, part_rows(ym), h1] + land[u, 1].astype(F32)).astype(BF16)
+        c[5].start()
+
+    def third(u):
+        c = units[u]
+        for number in (2, 3, 4, 5):
+            c[number].wait_recv()
+        rows = part_rows(y)
+        part[u % 2, rows, h0] += land[u, 4].astype(F32) + land[u, 2].astype(F32)
+        part[u % 2, rows, h1] += land[u, 5].astype(F32) + land[u, 3].astype(F32)
+        send[send_rows(u, y), others] = part[u % 2, rows, others].astype(BF16)
+        c[6].start()
+
+    def fourth(u):
+        c = units[u]
+        c[6].wait_recv()
+        rot_in[send_rows(u, y), mine] = (part[u % 2, part_rows(y), mine] + land_x[u].astype(F32)).astype(BF16)
+        for number in (7, 8, 9):
+            c[number].start()
+
+    def fifth(u):
+        c = units[u]
+        c[7].wait_recv()
+        c[10].start()
+        c[11].start()
+
+    def sixth(u):
+        c = units[u]
+        c[8].wait_recv()
+        c[12].start()
+        c[11].wait_recv()
+        c[13].start()
+
+    def last(u):
+        c = units[u]
+        for number in (9, 10, 12, 13):
+            c[number].wait_recv()
+
+    gradients_on()
+    loads[0].wait()
+    gather_a.wait(1)
+    gather_a.start(4, 5, 6)
+    gather_a.wait(2)
+    gather_a.start(8, 7)
+    gather_a.wait(3)
+    gather_a.start(9)
+    gradients_across()
+    loads[2].wait()
+    gather_a.wait(0, 4)
+    matmul(0)
+    second(0)
+    gather_a.wait(5)
+    gather_a.start(10)
+    gather_a.wait(6)
+    gather_a.start(12, 11)
+    third(0)
+    gather_a.wait(7, 10)
+    matmul(1)
+    fourth(0)
+    gather_a.wait(9, 11)
+    fifth(0)
+    second(1)
+    sixth(0)
+    third(1)
+    matmul(2)
+    gather_a.wait(8)
+    gather_a.start(13)
+    gather_a.wait(12)
+    gather_a.start(14)
+    fourth(1)
+    out_matmul()
+    second(2)
+    out_core()
+    fifth(1)
+    gather_a.wait(13, 14)
+    third(2)
+    sixth(1)
+    matmul(3)
+    fourth(2)
+    out_z()
+    fifth(2)
+    second(3)
+    sixth(2)
+    out_sum()
+    third(3)
+    out_final()
+    fourth(3)
+    gather_f.wait(1)
+    gather_f.start(4, 5, 6)
+    gather_f.wait(2)
+    gather_f.start(8, 7)
+    gather_f.wait(3)
+    gather_f.start(9)
+    fifth(3)
+    gather_f.wait(5)
+    gather_f.start(10)
+    gather_f.wait(6)
+    gather_f.start(12, 11)
+    sixth(3)
+    gather_f.wait(8)
+    gather_f.start(13)
+    gather_f.wait(12)
+    gather_f.start(14)
+    gather_f.wait(0, 4, 7, 9, 10, 11, 13, 14)
+    out_store = pltpu.make_async_copy(rot_out, rot_out_hbm, local.at[4])
+    out_store.start()
+    for u in range(4):
+        last(u)
+    in_store = pltpu.make_async_copy(rot_in, rot_in_hbm, local.at[5])
+    in_store.start()
+    gather_a.finish()
+    gather_f.finish()
+    for copy in d + [e0, e_x] + e:
+        copy.wait_send()
+    for c in units:
+        for copy in c:
+            copy.wait_send()
+    out_store.wait()
+    in_store.wait()
+
+
+def rotate(activations, gradients, basis_in, basis_out):
+    anywhere = pl.BlockSpec(memory_space=pl.ANY)
+    dma = pltpu.SemaphoreType.DMA
+    return pl.pallas_call(
+        rotate_kernel,
+        out_shape=(jax.ShapeDtypeStruct((1280, 1792), BF16), jax.ShapeDtypeStruct((1280, 1024), BF16)),
+        in_specs=[anywhere] * 4,
+        out_specs=(anywhere, anywhere),
+        scratch_shapes=[
+            pltpu.VMEM((1280, 3584), BF16),
+            pltpu.VMEM((3584, 1792), BF16),
+            pltpu.VMEM((2, 320, 1792), F32),
+            pltpu.VMEM((1280, 1792), BF16),
+            pltpu.VMEM((4, 6, 80, 896), BF16),
+            pltpu.VMEM((4, 80, 896), BF16),
+            pltpu.VMEM((1280, 1792), BF16),
+            pltpu.VMEM((1280, 512), BF16),
+            pltpu.VMEM((512, 1024), BF16),
+            pltpu.VMEM((1280, 1024), F32),
+            pltpu.VMEM((640, 1024), F32),
+            pltpu.VMEM((6, 160, 512), F32),
+            pltpu.VMEM((80, 1024), F32),
+            pltpu.VMEM((1280, 1024), BF16),
+            dma((15,)), dma((15,)),
+            dma((8,)), dma((8,)),
+            dma((8,)), dma((8,)),
+            dma((15,)), dma((15,)),
+            dma((4, 14)), dma((4, 14)),
+            dma((6,)),
+        ],
+        compiler_params=pltpu.CompilerParams(
+            collective_id=0, has_side_effects=True, vmem_limit_bytes=60 * 2**20
+        ),
+        cost_estimate=pl.CostEstimate(flops=18 * 10**9, bytes_accessed=22 * 10**6, transcendentals=0),
+    )(activations, gradients, basis_in, basis_out)
 
 
 def on_device(activations, gradients, basis_in, basis_out, eigen_damped, pair_ids):
     pair_rows = pair_ids.shape[0]
-    partial_in = jnp.dot(
-        lax.all_gather(activations, "col", axis=0, tiled=True),
-        basis_in,
-        preferred_element_type=jnp.float32,
-    )
-    rotated_in = lax.psum(partial_in, "row").astype(jnp.bfloat16)
-    partial_out = jnp.dot(
-        lax.all_gather(gradients, "row", axis=0, tiled=True),
-        basis_out,
-        preferred_element_type=jnp.float32,
-    )
-    rotated_out = lax.psum(partial_out, "col").astype(jnp.bfloat16)
+    rotated_in, rotated_out = rotate(activations, gradients, basis_in, basis_out)
     pair_in = rotated_in[:pair_rows]
     pair_out = rotated_out[:pair_rows]
     query_in = rotated_in[pair_rows:]

time: 510 us -> 238 us (0.47)
  blocking collectives: 401 us -> 63.9 us
  Pallas kernels: 0 us -> 138 us
  waiting for transfers between devices: 30.3 us -> 0 us
  matrix products: 48.1 us -> 18.8 us
  between operations: 21.1 us -> 7.72 us
    psum x2 -> x0, blocking collectives: 331 us -> none  [the longest x1 179 us: on_device(): rotated_in = lax.psum(partial_in, 'row').astype(jnp.bfloat16)]
    pallas_call x0 -> x1, Pallas kernels: none -> 138 us  [rotate(): pl.pallas_call(rotate_kernel, out_shape=(jax.ShapeDtypeStruct((1280, 1792...]
    dot_general x2 -> x0, matrix products: 29.2 us -> none  [the longest x1 24 us: on_device(): jnp.dot(lax.all_gather(activations, 'col', axis=0, tiled=True), basis_in,...]
    all_gather x2 -> x0, waiting for transfers between devices: 28.9 us -> none  [the longest x1 28.9 us: on_device(): lax.all_gather(gradients, 'row', axis=0, tiled=True)]
    psum x1, blocking collectives: 70.1 us -> 63.9 us  [on_device(): return lax.psum(partial_scores, ('row', 'col'))]
  transfers between devices with their start and end apart: 2 -> 0, of which waited for: 1 -> 0; matrix products, arithmetic and copies ran while one was open for 2% -> 0% of each run, Pallas kernels for 0% -> 0%
where the time goes in v1:
time: 238 us
  Pallas kernels  138 us (58%)
  blocking collectives  63.9 us (27%)
  matrix products  18.8 us (8%)
  between operations  7.72 us (3%)
  local copies, waits for them, and re-layouts  6.33 us (3%)
  other arithmetic  2.99 us (1%)
    pallas_call x1, Pallas kernels, rotate(): pl.pallas_call(rotate_kernel, out_shape=(jax.ShapeDtypeStruct((1280, 1792...  138 us
    psum x1, blocking collectives, on_device(): return lax.psum(partial_scores, ('row', 'col'))  63.9 us
    dot_general x4, matrix products, on_device(): lax.dot_general(window_out, window_in, (((0,), (0,)), ((), ())), preferre...  12.9 us
    dot_general x1, matrix products, on_device(): jnp.einsum('pif,sf->pis', scaled, query_in, preferred_element_type=jnp.fl...  5.91 us

profile of v1, /device:TPU:1, one launch (start us, length us, event | category | flops | bytes accessed | tf_op | source)
XLA Modules:
  0.0 238.0 jit_solution(17372505977490007349)
XLA Ops:
  0.0 0.8 convert_reduce_fusion
  0.8 0.7 fusion.45
  9.1 0.9 dynamic-slice_compare_fusion.3
  10.0 138.3 %shard_map.64 = (bf16[1280,1792]{1,0:T(8,128)(2,1)}, bf16[1280,1024]{1,0:T(8,128)(2,1)}) custom-call(bf16[80,3584]{1,0:T(8,128)(2,1)} %act.1, bf16[160,512]{1,0:T(8,128)(2,1)} %grad.1, bf16[3584,1792]{1,0:T(8,128)(2,1)} %basis_in.1, bf16[512,1024]{1,0:T(8,128)(2,1)} %basis_out.1), custom_call_target="tpu_custom_call" | custom-call | flops 17999998976 | bytes 22000000 | tf_op jit(solution)/shard_map/pallas_call | solution.py:412
  148.3 1.1 convert_bitcast_fusion
  149.4 1.8 slice.25
  151.2 1.3 copy.9
  152.5 0.0 slice-start
  152.5 2.4 %slice.26 = bf16[1024,1792]{1,0:T(8,128)(2,1)S(1)} slice(bf16[1280,1792]{1,0:T(8,128)(2,1)} %get-tuple-element.8), slice={[0:1024], [0:1792]} | slice | bytes 7340032 | tf_op jit(solution)/shard_map/slice | solution.py:449
  155.0 0.0 slice-start.1
  155.0 5.5 %fusion.11 = bf16[1,1024,1792]{2,1,0:T(8,128)(2,1)S(1)} fusion(f32[1024,1792]{1,0:T(8,128)} %param.10, bf16[1024,1792]{1,0:T(8,128)(2,1)S(1)} %slice.26, s32[]{:T(128)S(6)} %select_n.39, bf16[1024,1024]{1,0:T(8,128)(2,1)S(1)} %slice.25, pred[384]{0:T(512)(128)(4,1)S(1)} %get-tuple-element.11), kind=kOutput, calls=%fused_computation.16 | convolution fusion | flops 1413349376 | bytes 13174272 | tf_op jit(solution)/shard_map/dot_general | solution.py:464
  160.5 0.0 slice-done
  160.5 0.0 slice-done.1
  160.5 2.5 %fusion.10 = bf16[1,1024,1792]{2,1,0:T(8,128)(2,1)S(1)} fusion(f32[1024,1792]{1,0:T(8,128)S(1)} %bitcast.18, bf16[1024,1792]{1,0:T(8,128)(2,1)S(1)} %slice.26, s32[]{:T(128)S(6)} %select_n.37, bf16[1024,1024]{1,0:T(8,128)(2,1)S(1)} %slice.25, pred[384]{0:T(512)(128)(4,1)S(1)} %get-tuple-element.12), kind=kOutput, calls=%fused_computation.15 | convolution fusion | flops 1413349376 | bytes 13174272 | tf_op jit(solution)/shard_map/dot_general | solution.py:464
  163.0 2.5 %fusion.9 = bf16[1,1024,1792]{2,1,0:T(8,128)(2,1)S(1)} fusion(f32[1024,1792]{1,0:T(8,128)S(1)} %bitcast.18, bf16[1024,1792]{1,0:T(8,128)(2,1)S(1)} %slice.26, s32[]{:T(128)S(6)} %select_n.35, bf16[1024,1024]{1,0:T(8,128)(2,1)S(1)} %slice.25, pred[384]{0:T(512)(128)(4,1)S(1)} %get-tuple-element.10), kind=kOutput, calls=%fused_computation.14 | convolution fusion | flops 1413349376 | bytes 13174272 | tf_op jit(solution)/shard_map/dot_general | solution.py:464
  165.5 0.0 copy-start
  165.5 2.5 %fusion.8 = bf16[1,1024,1792]{2,1,0:T(8,128)(2,1)S(1)} fusion(f32[1024,1792]{1,0:T(8,128)S(1)} %bitcast.18, bf16[1024,1792]{1,0:T(8,128)(2,1)S(1)} %slice.26, s32[]{:T(128)S(6)} %select_n.33, bf16[1024,1024]{1,0:T(8,128)(2,1)S(1)} %slice.25, pred[384]{0:T(512)(128)(4,1)S(1)} %get-tuple-element.9), kind=kOutput, calls=%fused_computation.13 | convolution fusion | flops 1413349376 | bytes 13174272 | tf_op jit(solution)/shard_map/dot_general | solution.py:464
  167.9 0.0 copy-done
  167.9 5.9 %multiply_reduce_fusion = f32[4,256]{1,0:T(4,128)S(1)} fusion(bf16[1,1024,1792]{2,1,0:T(8,128)(2,1)S(1)} %fusion.11, bf16[1,1024,1792]{2,1,0:T(8,128)(2,1)S(1)} %fusion.10, bf16[1,1024,1792]{2,1,0:T(8,128)(2,1)S(1)} %fusion.9, bf16[1,1024,1792]{2,1,0:T(8,128)(2,1)S(1)} %fusion.8, f32[1024,256]{1,0:T(8,128)S(1)} %copy-done, ...), kind=kOutput, calls=%fused_computation.12 | convolution fusion | flops 3782212608 | bytes 16650240 | tf_op jit(solution)/shard_map/pif,sf->pis/dot_general | solution.py:469
  173.9 0.1 reshape.9
  174.0 0.1 reduce_sum.29
  174.1 63.9 %psum.7 = f32[4,64]{1,0:T(4,128)} all-reduce(f32[4,64]{1,0:T(4,128)S(1)} %reduce_sum.29), channel_id=1, replica_groups=mesh['row'=8,'col'=16] {'row','col'}, use_global_device_ids=true, to_apply=%region_3.4 | all-reduce | flops 256 | bytes 2048 | tf_op jit(solution)/shard_map/psum | solution.py:472
  (1 shorter events, 0.0 us)
Async XLA Ops:
  152.5 7.9 %slice-start = ((s8[7340032]{0:T(1024)(128)(4,1)}), s8[4194304]{0:T(1024)(128)(4,1)S(1)}, s32[]{:S(2)}) async-start(s8[7340032]{0:T(1024)(128)(4,1)} %bitcast.17), calls=%async_computation | async-start | bytes 8388608
  155.0 5.5 %slice-start.1 = ((s8[7340032]{0:T(1024)(128)(4,1)}), s8[3145728]{0:T(1024)(128)(4,1)S(1)}, s32[]{:S(2)}) async-start(s8[7340032]{0:T(1024)(128)(4,1)} %bitcast.17), calls=%async_computation.1 | async-start | bytes 6291456
  165.5 2.5 %copy-start = (f32[1024,256]{1,0:T(8,128)S(1)}, f32[1024,256]{1,0:T(8,128)}, u32[]{:S(2)}) copy-start(f32[1024,256]{1,0:T(8,128)} %copy.9) | copy-start | bytes 3145732

commit v2 on v0

v2 whole, which is shorter than its diff:
```python
import functools

import jax
import jax.numpy as jnp
from jax import lax
from jax.experimental import pallas as pl
from jax.experimental.pallas import tpu as pltpu
from jax.sharding import PartitionSpec as P

PAIRS = 4
QLEN = 4
WINDOWS = ((0, 384, 0), (0, 768, 384), (256, 1024, 1152), (640, 1024, 1920))
QUERY_AT = 2304
HALF = 896
SLOTS = 5
MESH = pl.DeviceIdType.MESH
BF16 = jnp.bfloat16
F32 = jnp.float32


def aligned(start, multiple, size):
    return pl.ds(pl.multiple_of(start, multiple), size)


class Place:
    def __init__(self):
        row, col = lax.axis_index("row"), lax.axis_index("col")
        self.xlo, self.y = row // 4, lax.rem(row, 4)
        self.z, self.xhi, self.core = col // 4, lax.rem(col // 2, 2), lax.rem(col, 2)

    def at(self, xlo=None, y=None, z=None, xhi=None, core=None):
        xlo = self.xlo if xlo is None else xlo
        y = self.y if y is None else y
        z = self.z if z is None else z
        xhi = self.xhi if xhi is None else xhi
        core = self.core if core is None else core
        return (xlo * 4 + y, z * 4 + xhi * 2 + core)


def remote(src, dst, sends, recvs, number, device):
    return pltpu.make_async_remote_copy(
        src_ref=src,
        dst_ref=dst,
        send_sem=sends.at[number],
        recv_sem=recvs.at[number],
        device_id=device,
        device_id_type=MESH,
    )


class Gather:
    def __init__(self, place, buf, slot, sends, recvs, first=None):
        zp, zm, z2 = (lax.rem(place.z + k, 4) for k in (1, 3, 2))
        xhi, other = place.xhi, 1 - place.xhi
        core, twin = place.core, 1 - place.core
        to_core, to_xhi = place.at(core=twin), place.at(xhi=other)
        to_zp, to_zm = place.at(z=zp), place.at(z=zm)
        z = place.z
        plan = [
            (z, xhi, to_core), (z, xhi, to_xhi), (z, xhi, to_zp), (z, xhi, to_zm),
            (z, other, to_core), (z, other, to_zp), (z, other, to_zm),
            (zm, xhi, to_core), (zm, xhi, to_zp), (zp, xhi, to_core),
            (zm, other, to_core), (zp, other, to_core), (zp, other, to_zm),
            (z2, xhi, to_core), (z2, other, to_core),
        ]
        self.copies = []
        for number, (from_z, from_x, device) in enumerate(plan):
            block = buf.at[slot(from_z, from_x, core)]
            src = first if number < 4 and first is not None else block
            self.copies.append(remote(src, block, sends, recvs, number, device))

    def start(self, *numbers):
        for number in numbers:
            self.copies[number].start()

    def wait(self, *numbers):
        for number in numbers:
            self.copies[number].wait_recv()

    def finish(self):
        for copy in self.copies:
            copy.wait_send()


ORDER = (
    ("rcp", "mm0", "Da", "Db", "sb0", "sa0", "A1", "A2", "A3", "Dc", "th0", "mm1", "sb1", "sa1", "A5", "A6"),
    ("th1", "Dx", "mm2", "outmm", "fo0", "fo1", "sb2", "mm3", "A8", "sa2", "mm5", "A12", "fa0", "fb0"),
    ("fa1", "fb1", "mm6", "sb3", "sa3", "mm4", "th2", "sa5", "sb5", "outa", "outb", "la0", "la1", "sb6"),
    ("fo2", "mm7", "th3", "sb4", "sa6", "sa4", "outsum", "th5", "fo3", "fa2", "sb7", "fb2", "sa7", "th6"),
    ("outfin", "th4", "fo5", "fb3", "fa3", "F2", "F3", "la2", "fo6", "th7", "fa5", "F1", "fb5", "F8", "la3"),
    ("fo4", "fa6", "fb6", "F5", "F6", "fo7", "la5", "fb4", "fa4", "F12", "la6", "Fdone", "prep", "fa7"),
    ("fb7", "la4", "fin0", "la7", "fin1"),
)


def kernel(
    act, grad, basis_in, basis_out, eigen, ids, scores,
    a_buf, b_buf, part, send, land, rot_in,
    g_buf, g_twin, bo_buf, bo_twin, part_out, land_z, land_h, rot_out,
    eig, acc, red_row, red_col,
    a_send, a_recv, d_send, d_recv, e_send, e_recv, f_send, f_recv, u_send, u_recv,
    r_send, r_recv, c_send, c_recv, local,
):
    me = Place()
    row, col = lax.axis_index("row"), lax.axis_index("col")
    xlo, y, z, xhi, core = me.xlo, me.y, me.z, me.xhi, me.core
    yp, ym, y2 = (lax.rem(y + k, 4) for k in (1, 3, 2))
    zp, zm, z2 = (lax.rem(z + k, 4) for k in (1, 3, 2))
    to_yp, to_ym = me.at(y=yp), me.at(y=ym)
    to_zp, to_zm = me.at(z=zp), me.at(z=zm)
    to_xlo, to_xhi, to_core = me.at(xlo=1 - xlo), me.at(xhi=1 - xhi), me.at(core=1 - core)
    row_mates = [(lax.rem(row + k, 8), col) for k in range(1, 8)]
    col_mates = [(row, lax.rem(col + k, 16)) for k in range(1, 16)]

    loads = {
        "act": pltpu.make_async_copy(act, a_buf.at[aligned(80 * (4 * z + 2 * xhi + core), 80, 80)], local.at[0]),
        "grad": pltpu.make_async_copy(grad, g_buf.at[aligned(160 * (4 * xlo + y), 160, 160)], local.at[1]),
        "basis_in": pltpu.make_async_copy(basis_in, b_buf, local.at[2]),
        "basis_out": pltpu.make_async_copy(basis_out, bo_buf, local.at[3]),
        "eigen": pltpu.make_async_copy(eigen, eig, local.at[4]),
    }
    for load in loads.values():
        load.start()

    barrier = pltpu.get_barrier_semaphore()
    for mate in row_mates + col_mates:
        pl.semaphore_signal(barrier, inc=1, device_id=mate, device_id_type=MESH)
    pl.semaphore_wait(barrier, len(row_mates) + len(col_mates))

    ops = {}

    gather_a = Gather(
        me, a_buf, lambda gz, gx, gc: aligned(80 * (4 * gz + 2 * gx + gc), 80, 80), a_send, a_recv, act
    )
    gather_f = Gather(
        me, rot_out, lambda gz, gx, gc: aligned(640 * gc + 160 * gz + 80 * gx, 80, 80), f_send, f_recv
    )
    onward = {1: (5, 6, 4), 2: (8, 7), 3: (9,), 5: (10,), 6: (12, 11), 8: (13,), 12: (14,)}

    def forward(gather, number):
        gather.wait(number)
        gather.start(*onward[number])

    for number in onward:
        ops["A%d" % number] = functools.partial(forward, gather_a, number)
        ops["F%d" % number] = functools.partial(forward, gather_f, number)

    def g_slot(gy, gx):
        return aligned(160 * (4 * gx + gy), 160, 160)

    def d_copy(number, rows, device, src=None):
        block = g_buf.at[rows]
        return remote(block if src is None else src, block, d_send, d_recv, number, device)

    d = [
        d_copy(0, g_slot(y, xlo), to_yp, grad),
        d_copy(1, g_slot(y, xlo), to_ym, grad),
        d_copy(2, g_slot(y, xlo), to_xlo, grad),
        d_copy(3, aligned(160 * (4 * xlo + ym), 80, 80), to_yp),
        d_copy(4, g_slot(ym, xlo), to_xlo),
        d_copy(5, aligned(160 * (4 * xlo + yp) + 80, 80, 80), to_ym),
        d_copy(6, g_slot(yp, xlo), to_xlo),
        d_copy(7, g_slot(y2, xlo), to_xlo),
        remote(g_buf.at[aligned(640 * (1 - core), 640, 640)], g_twin, d_send, d_recv, 8, to_core),
        remote(basis_out, bo_twin, d_send, d_recv, 9, to_core),
    ]

    def gradients_a():
        d[0].wait_recv()
        d[3].start()

    def gradients_b():
        d[1].wait_recv()
        d[5].start()

    def gradients_c():
        d[3].wait_recv()
        d[5].wait_recv()
        for number in (2, 4, 6, 7):
            d[number].start()

    def gradients_x():
        for number in (2, 4, 6, 7):
            d[number].wait_recv()
        loads["grad"].wait()
        d[8].start()

    ops.update(Da=gradients_a, Db=gradients_b, Dc=gradients_c, Dx=gradients_x)

    def e_rows(ez):
        return aligned(160 * ez, 160, 160)

    left, right = pl.ds(0, 512), pl.ds(512, 512)
    e = [
        remote(part_out.at[e_rows(z2), left], land_z.at[0], e_send, e_recv, 0, to_zp),
        remote(part_out.at[e_rows(z2), right], land_z.at[1], e_send, e_recv, 1, to_zm),
        remote(part_out.at[e_rows(zm), left], land_z.at[2], e_send, e_recv, 2, to_zm),
        remote(part_out.at[e_rows(zp), right], land_z.at[3], e_send, e_recv, 3, to_zp),
        remote(part_out.at[e_rows(zp), left], land_z.at[4], e_send, e_recv, 4, to_zp),
        remote(part_out.at[e_rows(zm), right], land_z.at[5], e_send, e_recv, 5, to_zm),
        remote(part_out.at[aligned(160 * z + 80 * (1 - xhi), 80, 80)], land_h, e_send, e_recv, 6, to_xhi),
    ]

    def out_matmul():
        loads["basis_out"].wait()
        d[8].wait_recv()
        d[9].wait_recv()

        @pl.loop(0, 4)
        def _(n):
            rows = aligned(160 * n, 160, 160)
            part_out[rows, :] = jnp.dot(
                g_buf[aligned(640 * core + 160 * n, 160, 160), :], bo_buf[...], preferred_element_type=F32
            ) + jnp.dot(g_twin[rows, :], bo_twin[...], preferred_element_type=F32)

        for copy in e[:4]:
            copy.start()

    def out_a():
        e[0].wait_recv()
        part_out[e_rows(zp), left] += land_z[0]
        e[4].start()

    def out_b():
        e[1].wait_recv()
        part_out[e_rows(zm), right] += land_z[1]
        e[5].start()

    def out_sum():
        for copy in e[2:6]:
            copy.wait_recv()
        part_out[e_rows(z), left] += land_z[4] + land_z[2]
        part_out[e_rows(z), right] += land_z[5] + land_z[3]
        e[6].start()

    def out_final():
        e[6].wait_recv()
        rot_out[aligned(640 * core + 160 * z + 80 * xhi, 80, 80), :] = (
            part_out[aligned(160 * z + 80 * xhi, 80, 80), :] + land_h[...]
        ).astype(BF16)
        gather_f.start(1, 2, 3, 0)

    def out_done():
        gather_f.wait(0, 4, 7, 9, 10, 11, 13, 14)

    ops.update(outmm=out_matmul, outa=out_a, outb=out_b, outsum=out_sum, outfin=out_final, Fdone=out_done)

    class Unit:
        def __init__(self, u):
            self.u, self.slot = u, u % SLOTS
            if u < 2:
                self.start = 160 * (2 * z + (xhi, 1 - xhi)[u])
                self.need = ((0,), (4,))[u]
            else:
                self.start = 320 * (zm, zp, z2)[(u - 2) % 3]
                self.need = ((7, 10), (9, 11), (13, 14))[(u - 2) % 3] if u < 5 else ()
            big, small = pl.ds(0, 48), pl.ds(48, 32)
            self.h = (big, small)
            if u % 2 == 0:
                self.up, self.down, to_up, to_down = yp, ym, to_yp, to_ym
                onward_a, onward_b = (48, 32), (0, 48)
            else:
                self.up, self.down, to_up, to_down = ym, yp, to_ym, to_yp
                onward_a, onward_b = (0, 48), (48, 32)

            def term(number, owner, rows, where, device):
                return remote(
                    send.at[u, owner, rows], land.at[u, where, rows], u_send.at[u], u_recv.at[u], number, device
                )

            def spread(number, owner, device, offset=0, count=80):
                block = rot_in.at[self.place(owner, offset, count)]
                return remote(block, block, u_send.at[u], u_recv.at[u], number, device)

            self.copies = [
                term(0, y2, big, 0, to_up),
                term(1, y2, small, 0, to_down),
                term(2, self.down, big, 1, to_down),
                term(3, self.up, small, 1, to_up),
                term(4, self.up, big, 2, to_up),
                term(5, self.down, small, 2, to_down),
                remote(send.at[u, y], land.at[u, 3], u_send.at[u], u_recv.at[u], 6, to_xlo),
                spread(7, y, to_yp),
                spread(8, y, to_ym),
                spread(9, ym, to_yp, *onward_a),
                spread(10, yp, to_ym, *onward_b),
            ]

        def place(self, owner, offset=0, count=80):
            if self.u < 2:
                rows = aligned(self.start + 80 * (owner // 2) + offset, 16, count)
                return rows, aligned(HALF * lax.rem(owner, 2), 128, HALF)
            return aligned(self.start + 80 * owner + offset, 16, count), pl.ds(HALF * ((self.u - 2) // 3), HALF)

        def matmul(self):
            if self.u == 0:
                loads["act"].wait()
                loads["basis_in"].wait()
            gather_a.wait(*self.need)
            if self.u < 2:
                rows = aligned(self.start, 160, 160)

                @pl.loop(0, 2)
                def _(n):
                    block = jnp.dot(
                        a_buf[rows, :], b_buf[:, aligned(HALF * n, HALF, HALF)], preferred_element_type=F32
                    )
                    for half in range(2):
                        piece = block[80 * half:80 * half + 80]
                        part[self.slot, 2 * half + n] = piece
                        send[self.u, 2 * half + n] = piece.astype(BF16)
            else:
                block = jnp.dot(
                    a_buf[aligned(self.start, 320, 320), :],
                    b_buf[:, HALF * ((self.u - 2) // 3):HALF * ((self.u - 2) // 3) + HALF],
                    preferred_element_type=F32,
                )
                for owner in range(4):
                    piece = block[80 * owner:80 * owner + 80]
                    part[self.slot, owner] = piece
                    send[self.u, owner] = piece.astype(BF16)
            for copy in self.copies[:4]:
                copy.start()

        def second(self, number):
            owner, rows = ((self.up, self.h[0]), (self.down, self.h[1]))[number]
            self.copies[number].wait_recv()
            send[self.u, owner, rows] = (
                part[self.slot, owner, rows] + land[self.u, 0, rows].astype(F32)
            ).astype(BF16)
            self.copies[4 + number].start()

        def third(self):
            for number in (2, 3, 4, 5):
                self.copies[number].wait_recv()
            total = part[self.slot, y] + (land[self.u, 1].astype(F32) + land[self.u, 2].astype(F32))
            part[self.slot, y] = total
            send[self.u, y] = total.astype(BF16)
            self.copies[6].start()

        def fourth(self):
            self.copies[6].wait_recv()
            rot_in[self.place(y)] = (part[self.slot, y] + land[self.u, 3].astype(F32)).astype(BF16)
            self.copies[7].start()
            self.copies[8].start()

        def spread_on(self, number):
            self.copies[7 + number].wait_recv()
            self.copies[9 + number].start()

        def last(self):
            self.copies[9].wait_recv()
            self.copies[10].wait_recv()

    units = [Unit(u) for u in range(8)]
    for u, unit in enumerate(units):
        ops["mm%d" % u] = unit.matmul
        ops["sa%d" % u] = functools.partial(unit.second, 0)
        ops["sb%d" % u] = functools.partial(unit.second, 1)
        ops["th%d" % u] = unit.third
        ops["fo%d" % u] = unit.fourth
        ops["fa%d" % u] = functools.partial(unit.spread_on, 0)
        ops["fb%d" % u] = functools.partial(unit.spread_on, 1)
        ops["la%d" % u] = unit.last

    def reciprocal():
        loads["eigen"].wait()

        @pl.loop(0, 16)
        def _(n):
            rows = aligned(64 * n, 64, 64)
            eig[rows, :] = 1.0 / eig[rows, :]

    def prepare():
        gather_a.finish()

        @pl.loop(0, 4)
        def _(n):
            rows = aligned(256 * n, 256, 256)
            turned = rot_out[:, rows].astype(F32).T
            for p, (first, last, at) in enumerate(WINDOWS):
                kept = jnp.where(ids[0:1, first:last] == p, turned[:, first:last], 0.0)
                a_buf[rows, at:at + last - first] = kept.astype(BF16)
            a_buf[rows, QUERY_AT:QUERY_AT + 256] = turned[:, 1024:1280].astype(BF16)

        acc[...] = jnp.zeros_like(acc)

    def final(half):
        cols = slice(HALF * half, HALF * half + HALF)
        for p, (first, last, at) in enumerate(WINDOWS):

            @pl.loop(0, 4)
            def _(n):
                rows = aligned(256 * n, 256, 256)
                pair_block = jnp.dot(
                    a_buf[rows, at:at + last - first], rot_in[first:last, cols], preferred_element_type=F32
                )
                scaled = (pair_block * eig[rows, cols]).astype(BF16)
                mapped = lax.dot_general(
                    scaled, rot_in[1024:1280, cols], (((1,), (1,)), ((), ())), preferred_element_type=F32
                )
                query = a_buf[rows, QUERY_AT:QUERY_AT + 256].astype(F32)
                acc[p:p + 1, :] += jnp.sum(mapped * query, axis=0, keepdims=True)

    ops.update(rcp=reciprocal, prep=prepare, fin0=functools.partial(final, 0), fin1=functools.partial(final, 1))

    gather_a.start(1, 2, 3, 0)
    d[0].start()
    d[1].start()
    d[9].start()
    for names in ORDER:
        for name in names:
            ops[name]()

    token = lax.broadcasted_iota(jnp.int32, (256, 128), 0)
    query = lax.broadcasted_iota(jnp.int32, (256, 128), 1)
    pick = jnp.where(token // QLEN == query, 1.0, 0.0)
    red_row[row] = jnp.dot(acc[...], pick, precision=lax.Precision.HIGHEST, preferred_element_type=F32)

    def everyone(red, position, mates, sends, recvs):
        copies = []
        for k, mate in enumerate(mates):
            copies.append(remote(red.at[position], red.at[position], sends, recvs, k, mate))
        for copy in copies:
            copy.start()
        for copy in copies:
            copy.wait_recv()
        return copies

    row_copies = everyone(red_row, row, row_mates, r_send, r_recv)
    red_col[col] = jnp.sum(red_row[...], axis=0)
    col_copies = everyone(red_col, col, col_mates, c_send, c_recv)
    scores[...] = jnp.sum(red_col[...], axis=0)[:PAIRS, :64]

    gather_f.finish()
    for copy in d + e + row_copies + col_copies:
        copy.wait_send()
    for unit in units:
        for copy in unit.copies:
            copy.wait_send()


def on_device(activations, gradients, basis_in, basis_out, eigen_damped, pair_ids):
    anywhere = pl.BlockSpec(memory_space=pl.ANY)
    vmem = pl.BlockSpec(memory_space=pltpu.VMEM)
    dma = pltpu.SemaphoreType.DMA
    return pl.pallas_call(
        kernel,
        out_shape=jax.ShapeDtypeStruct((PAIRS, 64), F32),
        in_specs=[anywhere] * 5 + [vmem],
        out_specs=vmem,
        scratch_shapes=[
            pltpu.VMEM((1280, 3584), BF16),
            pltpu.VMEM((3584, 1792), BF16),
            pltpu.VMEM((SLOTS, 4, 80, HALF), F32),
            pltpu.VMEM((8, 4, 80, HALF), BF16),
            pltpu.VMEM((8, 4, 80, HALF), BF16),
            pltpu.VMEM((1280, 1792), BF16),
            pltpu.VMEM((1280, 512), BF16),
            pltpu.VMEM((640, 512), BF16),
            pltpu.VMEM((512, 1024), BF16),
            pltpu.VMEM((512, 1024), BF16),
            pltpu.VMEM((640, 1024), F32),
            pltpu.VMEM((6, 160, 512), F32),
            pltpu.VMEM((80, 1024), F32),
            pltpu.VMEM((1280, 1024), BF16),
            pltpu.VMEM((1024, 1792), F32),
            pltpu.VMEM((8, 256), F32),
            pltpu.VMEM((8, 8, 128), F32),
            pltpu.VMEM((16, 8, 128), F32),
            dma((15,)), dma((15,)),
            dma((10,)), dma((10,)),
            dma((7,)), dma((7,)),
            dma((15,)), dma((15,)),
            dma((8, 11)), dma((8, 11)),
            dma((7,)), dma((7,)),
            dma((15,)), dma((15,)),
            dma((5,)),
        ],
        compiler_params=pltpu.CompilerParams(
            collective_id=0, has_side_effects=True, vmem_limit_bytes=63 * 2**20
        ),
        cost_estimate=pl.CostEstimate(flops=28 * 10**9, bytes_accessed=22 * 10**6, transcendentals=0),
    )(activations, gradients, basis_in, basis_out, eigen_damped, pair_ids.reshape(1, 1024))


def solution(mesh):
    return jax.shard_map(
        on_device,
        mesh=mesh,
        in_specs=(
            P("col", "row"),
            P("row", "col"),
            P("row", "col"),
            P("col", "row"),
            P("row", "col"),
            P(),
        ),
        out_specs=P(),
        check_vma=False,
    )
```

time: 510 us -> 149 us (0.29)
  blocking collectives: 401 us -> 0 us
  Pallas kernels: 0 us -> 148 us
  matrix products: 48.1 us -> 0 us
  waiting for transfers between devices: 30.3 us -> 0 us
  between operations: 21.1 us -> 0.01 us
    psum x3 -> x0, blocking collectives: 401 us -> none  [the longest x1 179 us: on_device(): rotated_in = lax.psum(partial_in, 'row').astype(jnp.bfloat16)]
    pallas_call x0 -> x1, Pallas kernels: none -> 148 us  [on_device(): pl.pallas_call(kernel, out_shape=jax.ShapeDtypeStruct((PAIRS, 64), F32),...]
    dot_general x7 -> x0, matrix products: 48.1 us -> none  [the longest x1 24 us: on_device(): jnp.dot(lax.all_gather(activations, 'col', axis=0, tiled=True), basis_in,...]
    all_gather x2 -> x0, waiting for transfers between devices: 28.9 us -> none  [the longest x1 28.9 us: on_device(): lax.all_gather(gradients, 'row', axis=0, tiled=True)]
  transfers between devices with their start and end apart: 2 -> 0, of which waited for: 1 -> 0; matrix products, arithmetic and copies ran while one was open for 2% -> 0% of each run, Pallas kernels for 0% -> 0%
where the time goes in v2:
time: 149 us
  Pallas kernels  148 us (99%)
    pallas_call x1, Pallas kernels, on_device(): pl.pallas_call(kernel, out_shape=jax.ShapeDtypeStruct((PAIRS, 64), F32),...  148 us

profile of v2, /device:TPU:1, one launch (start us, length us, event | category | flops | bytes accessed | tf_op | source)
XLA Modules:
  0.0 149.2 jit_solution(10560997019875575638)
XLA Ops:
  0.0 148.0 %shard_map.64 = f32[4,64]{1,0:T(4,128)} custom-call(bf16[80,3584]{1,0:T(8,128)(2,1)} %act.1, bf16[160,512]{1,0:T(8,128)(2,1)} %grad.1, bf16[3584,1792]{1,0:T(8,128)(2,1)} %basis_in.1, bf16[512,1024]{1,0:T(8,128)(2,1)} %basis_out.1, f32[1024,1792]{1,0:T(8,128)} %eigen.1, s32[1,1024]{1,0:T(1,128)} %bitcast.1), custom_call_target="tpu_custom_call" | custom-call | flops 28000000000 | bytes 22000000 | tf_op jit(solution)/shard_map/pallas_call | solution.py:447
  148.0 1.3 copy.8

commit v3 on v2

--- a/solution.py
+++ b/solution.py
@@ -83,13 +83,14 @@
 
 
 ORDER = (
-    ("rcp", "mm0", "Da", "Db", "sb0", "sa0", "A1", "A2", "A3", "Dc", "th0", "mm1", "sb1", "sa1", "A5", "A6"),
-    ("th1", "Dx", "mm2", "outmm", "fo0", "fo1", "sb2", "mm3", "A8", "sa2", "mm5", "A12", "fa0", "fb0"),
-    ("fa1", "fb1", "mm6", "sb3", "sa3", "mm4", "th2", "sa5", "sb5", "outa", "outb", "la0", "la1", "sb6"),
-    ("fo2", "mm7", "th3", "sb4", "sa6", "sa4", "outsum", "th5", "fo3", "fa2", "sb7", "fb2", "sa7", "th6"),
-    ("outfin", "th4", "fo5", "fb3", "fa3", "F2", "F3", "la2", "fo6", "th7", "fa5", "F1", "fb5", "F8", "la3"),
-    ("fo4", "fa6", "fb6", "F5", "F6", "fo7", "la5", "fb4", "fa4", "F12", "la6", "Fdone", "prep", "fa7"),
-    ("fb7", "la4", "fin0", "la7", "fin1"),
+    ("Ax", "Db", "Da", "mm0", "Dc2", "Dc4", "sb0", "A1", "Dc7", "sa0", "mm1", "Dc6", "rcp", "sb1", "A2", "th0"),
+    ("A3", "A6", "Dx", "sa1", "A5", "mm3", "mm2", "outmm", "sa3", "sb2", "A8", "th1", "sa2", "A12", "fo0", "sb3"),
+    ("mm5", "fo1", "th2", "outb", "sa5", "th3", "sb5", "outa", "fo2", "mm7", "mm4", "th5", "outsum", "fo3"),
+    ("sa4", "sb7", "sb4", "fb1", "mm6", "fa2", "sa7", "fo5", "outfin", "go5", "sb6", "sa6", "fa0", "fa1", "th4"),
+    ("th7", "fb2", "fb3", "F1", "fa5", "fb5", "fa3", "fb0", "F2", "fo4", "th6", "F3", "F6", "F8", "fo7", "la3"),
+    ("F5", "la1", "F12", "fo6", "fb4", "gb5", "fa4", "go6", "la2", "la5", "go7", "fa7", "la0", "Fdone", "prep"),
+    ("fa6", "ga5", "la4", "fb7", "fb6", "fin0", "ga6", "gb6", "la6", "la7", "gb7", "ga7", "fin1", "ka5", "ka6"),
+    ("ka7", "fin2"),
 )
 
 
@@ -144,6 +145,7 @@
     for number in onward:
         ops["A%d" % number] = functools.partial(forward, gather_a, number)
         ops["F%d" % number] = functools.partial(forward, gather_f, number)
+    ops["Ax"] = functools.partial(gather_a.start, 1)
 
     def g_slot(gy, gx):
         return aligned(160 * (4 * gx + gy), 160, 160)
@@ -173,11 +175,11 @@
         d[1].wait_recv()
         d[5].start()
 
-    def gradients_c():
-        d[3].wait_recv()
-        d[5].wait_recv()
-        for number in (2, 4, 6, 7):
-            d[number].start()
+    def gradients_across(number):
+        if number == 7:
+            d[3].wait_recv()
+            d[5].wait_recv()
+        d[number].start()
 
     def gradients_x():
         for number in (2, 4, 6, 7):
@@ -185,7 +187,9 @@
         loads["grad"].wait()
         d[8].start()
 
-    ops.update(Da=gradients_a, Db=gradients_b, Dc=gradients_c, Dx=gradients_x)
+    ops.update(Da=gradients_a, Db=gradients_b, Dx=gradients_x)
+    for number in (2, 4, 6, 7):
+        ops["Dc%d" % number] = functools.partial(gradients_across, number)
 
     def e_rows(ez):
         return aligned(160 * ez, 160, 160)
@@ -253,7 +257,7 @@
                 self.need = ((0,), (4,))[u]
             else:
                 self.start = 320 * (zm, zp, z2)[(u - 2) % 3]
-                self.need = ((7, 10), (9, 11), (13, 14))[(u - 2) % 3] if u < 5 else ()
+                self.need = ((7, 10), (9, 11), (13, 14))[(u - 2) % 3]
             big, small = pl.ds(0, 48), pl.ds(48, 32)
             self.h = (big, small)
             if u % 2 == 0:
@@ -268,8 +272,8 @@
                     send.at[u, owner, rows], land.at[u, where, rows], u_send.at[u], u_recv.at[u], number, device
                 )
 
-            def spread(number, owner, device, offset=0, count=80):
-                block = rot_in.at[self.place(owner, offset, count)]
+            def spread(number, owner, device, offset=0, count=80, piece=0):
+                block = rot_in.at[self.place(owner, offset, count, piece)]
                 return remote(block, block, u_send.at[u], u_recv.at[u], number, device)
 
             self.copies = [
@@ -280,23 +284,32 @@
                 term(4, self.up, big, 2, to_up),
                 term(5, self.down, small, 2, to_down),
                 remote(send.at[u, y], land.at[u, 3], u_send.at[u], u_recv.at[u], 6, to_xlo),
-                spread(7, y, to_yp),
-                spread(8, y, to_ym),
-                spread(9, ym, to_yp, *onward_a),
-                spread(10, yp, to_ym, *onward_b),
             ]
-
-        def place(self, owner, offset=0, count=80):
+            self.pieces = 2 if u >= 5 else 1
+            for piece in range(self.pieces):
+                number = 7 + 4 * piece
+                self.copies += [
+                    spread(number, y, to_yp, piece=piece),
+                    spread(number + 1, y, to_ym, piece=piece),
+                    spread(number + 2, ym, to_yp, *onward_a, piece=piece),
+                    spread(number + 3, yp, to_ym, *onward_b, piece=piece),
+                ]
+
+        def place(self, owner, offset=0, count=80, piece=None):
             if self.u < 2:
                 rows = aligned(self.start + 80 * (owner // 2) + offset, 16, count)
                 return rows, aligned(HALF * lax.rem(owner, 2), 128, HALF)
-            return aligned(self.start + 80 * owner + offset, 16, count), pl.ds(HALF * ((self.u - 2) // 3), HALF)
+            rows = aligned(self.start + 80 * owner + offset, 16, count)
+            if self.u < 5:
+                return rows, pl.ds(0, HALF)
+            return rows, (pl.ds(HALF, HALF), pl.ds(HALF, 384), pl.ds(HALF + 384, 512))[0 if piece is None else 1 + piece]
 
         def matmul(self):
             if self.u == 0:
                 loads["act"].wait()
                 loads["basis_in"].wait()
-            gather_a.wait(*self.need)
+            gather_a.wait(*[number for number in self.need if number not in arrived])
+            arrived.update(self.need)
             if self.u < 2:
                 rows = aligned(self.start, 160, 160)
 
@@ -341,17 +354,21 @@
         def fourth(self):
             self.copies[6].wait_recv()
             rot_in[self.place(y)] = (part[self.slot, y] + land[self.u, 3].astype(F32)).astype(BF16)
-            self.copies[7].start()
-            self.copies[8].start()
-
-        def spread_on(self, number):
-            self.copies[7 + number].wait_recv()
-            self.copies[9 + number].start()
-
-        def last(self):
-            self.copies[9].wait_recv()
-            self.copies[10].wait_recv()
-
+            self.give(0)
+
+        def give(self, piece):
+            self.copies[7 + 4 * piece].start()
+            self.copies[8 + 4 * piece].start()
+
+        def spread_on(self, piece, number):
+            self.copies[7 + 4 * piece + number].wait_recv()
+            self.copies[9 + 4 * piece + number].start()
+
+        def last(self, piece):
+            self.copies[9 + 4 * piece].wait_recv()
+            self.copies[10 + 4 * piece].wait_recv()
+
+    arrived = set()
     units = [Unit(u) for u in range(8)]
     for u, unit in enumerate(units):
         ops["mm%d" % u] = unit.matmul
@@ -359,9 +376,12 @@
         ops["sb%d" % u] = functools.partial(unit.second, 1)
         ops["th%d" % u] = unit.third
         ops["fo%d" % u] = unit.fourth
-        ops["fa%d" % u] = functools.partial(unit.spread_on, 0)
-        ops["fb%d" % u] = functools.partial(unit.spread_on, 1)
-        ops["la%d" % u] = unit.last
+        for piece in range(unit.pieces):
+            ops["fg"[piece] + "a%d" % u] = functools.partial(unit.spread_on, piece, 0)
+            ops["fg"[piece] + "b%d" % u] = functools.partial(unit.spread_on, piece, 1)
+            ops["lk"[piece] + "a%d" % u] = functools.partial(unit.last, piece)
+        if unit.pieces == 2:
+            ops["go%d" % u] = functools.partial(unit.give, 1)
 
     def reciprocal():
         loads["eigen"].wait()
@@ -385,26 +405,35 @@
 
         acc[...] = jnp.zeros_like(acc)
 
-    def final(half):
-        cols = slice(HALF * half, HALF * half + HALF)
-        for p, (first, last, at) in enumerate(WINDOWS):
-
-            @pl.loop(0, 4)
-            def _(n):
-                rows = aligned(256 * n, 256, 256)
-                pair_block = jnp.dot(
-                    a_buf[rows, at:at + last - first], rot_in[first:last, cols], preferred_element_type=F32
+    def final(chunks):
+        @pl.loop(0, 2)
+        def _(n):
+            rows = aligned(512 * n, 512, 512)
+            query = a_buf[rows, QUERY_AT:QUERY_AT + 256].astype(F32)
+            for chunk in chunks:
+                cols = slice(256 * chunk, 256 * chunk + 256)
+                inverse = eig[rows, cols]
+                scaled = []
+                for first, last, at in WINDOWS:
+                    pair_block = jnp.dot(
+                        a_buf[rows, at:at + last - first], rot_in[first:last, cols], preferred_element_type=F32
+                    )
+                    scaled.append((pair_block * inverse).astype(BF16))
+                mapped = lax.dot_general(
+                    jnp.concatenate(scaled, axis=0),
+                    rot_in[1024:1280, cols],
+                    (((1,), (1,)), ((), ())),
+                    preferred_element_type=F32,
                 )
-                scaled = (pair_block * eig[rows, cols]).astype(BF16)
-                mapped = lax.dot_general(
-                    scaled, rot_in[1024:1280, cols], (((1,), (1,)), ((), ())), preferred_element_type=F32
-                )
-                query = a_buf[rows, QUERY_AT:QUERY_AT + 256].astype(F32)
-                acc[p:p + 1, :] += jnp.sum(mapped * query, axis=0, keepdims=True)
-
-    ops.update(rcp=reciprocal, prep=prepare, fin0=functools.partial(final, 0), fin1=functools.partial(final, 1))
-
-    gather_a.start(1, 2, 3, 0)
+                for p in range(PAIRS):
+                    product = mapped[512 * p:512 * p + 512] * query
+                    acc[8 * p:8 * p + 8, :] += jnp.sum(product.reshape(64, 8, 256), axis=0)
+
+    ops.update(rcp=reciprocal, prep=prepare)
+    for number, chunks in enumerate(((0, 1, 2), (3, 4), (5, 6))):
+        ops["fin%d" % number] = functools.partial(final, chunks)
+
+    gather_a.start(2, 3, 0)
     d[0].start()
     d[1].start()
     d[9].start()
@@ -415,7 +444,9 @@
     token = lax.broadcasted_iota(jnp.int32, (256, 128), 0)
     query = lax.broadcasted_iota(jnp.int32, (256, 128), 1)
     pick = jnp.where(token // QLEN == query, 1.0, 0.0)
-    red_row[row] = jnp.dot(acc[...], pick, precision=lax.Precision.HIGHEST, preferred_element_type=F32)
+    per_token = jnp.sum(acc[...].reshape(PAIRS, 8, 256), axis=1)
+    red_row[row] = jnp.zeros((8, 128), F32)
+    red_row[row, :PAIRS] = jnp.dot(per_token, pick, precision=lax.Precision.HIGHEST, preferred_element_type=F32)
 
     def everyone(red, position, mates, sends, recvs):
         copies = []
@@ -465,14 +496,14 @@
             pltpu.VMEM((80, 1024), F32),
             pltpu.VMEM((1280, 1024), BF16),
             pltpu.VMEM((1024, 1792), F32),
-            pltpu.VMEM((8, 256), F32),
+            pltpu.VMEM((8 * PAIRS, 256), F32),
             pltpu.VMEM((8, 8, 128), F32),
             pltpu.VMEM((16, 8, 128), F32),
             dma((15,)), dma((15,)),
             dma((10,)), dma((10,)),
             dma((7,)), dma((7,)),
             dma((15,)), dma((15,)),
-            dma((8, 11)), dma((8, 11)),
+            dma((8, 15)), dma((8, 15)),
             dma((7,)), dma((7,)),
             dma((15,)), dma((15,)),
             dma((5,)),

time: 149 us -> 134 us (0.90)
  Pallas kernels: 148 us -> 133 us
    pallas_call x1, Pallas kernels: 148 us -> 133 us  [on_device(): pl.pallas_call(kernel, out_shape=jax.ShapeDtypeStruct((PAIRS, 64), F32),...]
where the time goes in v3:
time: 134 us
  Pallas kernels  133 us (99%)
    pallas_call x1, Pallas kernels, on_device(): pl.pallas_call(kernel, out_shape=jax.ShapeDtypeStruct((PAIRS, 64), F32),...  133 us

profile of v3, /device:TPU:1, one launch (start us, length us, event | category | flops | bytes accessed | tf_op | source)
XLA Modules:
  0.0 134.3 jit_solution(1162676411363541696)
XLA Ops:
  0.0 133.1 %shard_map.64 = f32[4,64]{1,0:T(4,128)} custom-call(bf16[80,3584]{1,0:T(8,128)(2,1)} %act.1, bf16[160,512]{1,0:T(8,128)(2,1)} %grad.1, bf16[3584,1792]{1,0:T(8,128)(2,1)} %basis_in.1, bf16[512,1024]{1,0:T(8,128)(2,1)} %basis_out.1, f32[1024,1792]{1,0:T(8,128)} %eigen.1, s32[1,1024]{1,0:T(1,128)} %bitcast.1), custom_call_target="tpu_custom_call" | custom-call | flops 28000000000 | bytes 22000000 | tf_op jit(solution)/shard_map/pallas_call | solution.py:478
  133.1 1.3 copy.8

commit v4 on v3

--- a/solution.py
+++ b/solution.py
@@ -83,14 +83,14 @@
 
 
 ORDER = (
-    ("Ax", "Db", "Da", "mm0", "Dc2", "Dc4", "sb0", "A1", "Dc7", "sa0", "mm1", "Dc6", "rcp", "sb1", "A2", "th0"),
-    ("A3", "A6", "Dx", "sa1", "A5", "mm3", "mm2", "outmm", "sa3", "sb2", "A8", "th1", "sa2", "A12", "fo0", "sb3"),
-    ("mm5", "fo1", "th2", "outb", "sa5", "th3", "sb5", "outa", "fo2", "mm7", "mm4", "th5", "outsum", "fo3"),
-    ("sa4", "sb7", "sb4", "fb1", "mm6", "fa2", "sa7", "fo5", "outfin", "go5", "sb6", "sa6", "fa0", "fa1", "th4"),
-    ("th7", "fb2", "fb3", "F1", "fa5", "fb5", "fa3", "fb0", "F2", "fo4", "th6", "F3", "F6", "F8", "fo7", "la3"),
-    ("F5", "la1", "F12", "fo6", "fb4", "gb5", "fa4", "go6", "la2", "la5", "go7", "fa7", "la0", "Fdone", "prep"),
-    ("fa6", "ga5", "la4", "fb7", "fb6", "fin0", "ga6", "gb6", "la6", "la7", "gb7", "ga7", "fin1", "ka5", "ka6"),
-    ("ka7", "fin2"),
+    ("Ax", "mm0", "Dc2", "Da", "sb0", "Db", "sa0", "A1", "A3", "th0", "Dc7", "A2", "Dc6", "mm1", "fo0", "mm3"),
+    ("mm2", "Dc4", "A6", "sb1", "fa0", "sa1", "A5", "fb0", "mm5", "Dx", "sa3", "sb3", "sb2", "mm4", "outmm0"),
+    ("la0", "sa2", "th1", "sa4", "sa5", "th3", "outmm1", "rcp", "A8", "sb5", "outa0", "A12", "th2", "fo1", "sb4"),
+    ("fo3", "th5", "mm6", "outb0", "fo2", "outb1", "th4", "fa1", "mm7", "sa6", "outa1", "sb6", "outsum0", "fb2"),
+    ("outsum1", "sb7", "outfin0", "fb1", "fa3", "fo5", "th6", "outfin1", "sa7", "fo4", "H2", "F3", "F1", "la1"),
+    ("H1", "fo6", "H8", "fb5", "H3", "fa5", "th7", "fa2", "fb3", "F2", "H6", "fb6", "F6", "fo7", "fa6", "H12"),
+    ("la3", "F8", "F5", "la5", "H5", "fb4", "la2", "F12", "fa4", "go7", "fa7", "fb7", "la6", "Fdone", "prep"),
+    ("la4", "fin0", "gb7", "la7", "ga7", "fin1", "ka7", "fin2"),
 )
 
 
@@ -116,13 +116,11 @@
     loads = {
         "act": pltpu.make_async_copy(act, a_buf.at[aligned(80 * (4 * z + 2 * xhi + core), 80, 80)], local.at[0]),
         "grad": pltpu.make_async_copy(grad, g_buf.at[aligned(160 * (4 * xlo + y), 160, 160)], local.at[1]),
-        "basis_in": pltpu.make_async_copy(basis_in, b_buf, local.at[2]),
+        "basis_in_0": pltpu.make_async_copy(basis_in.at[:, pl.ds(0, HALF)], b_buf.at[:, pl.ds(0, HALF)], local.at[2]),
+        "basis_in_1": pltpu.make_async_copy(basis_in.at[:, pl.ds(HALF, HALF)], b_buf.at[:, pl.ds(HALF, HALF)], local.at[5]),
         "basis_out": pltpu.make_async_copy(basis_out, bo_buf, local.at[3]),
         "eigen": pltpu.make_async_copy(eigen, eig, local.at[4]),
     }
-    for load in loads.values():
-        load.start()
-
     barrier = pltpu.get_barrier_semaphore()
     for mate in row_mates + col_mates:
         pl.semaphore_signal(barrier, inc=1, device_id=mate, device_id_type=MESH)
@@ -133,9 +131,13 @@
     gather_a = Gather(
         me, a_buf, lambda gz, gx, gc: aligned(80 * (4 * gz + 2 * gx + gc), 80, 80), a_send, a_recv, act
     )
-    gather_f = Gather(
-        me, rot_out, lambda gz, gx, gc: aligned(640 * gc + 160 * gz + 80 * gx, 80, 80), f_send, f_recv
-    )
+    gather_out = [
+        Gather(
+            me, rot_out.at[:, pl.ds(512 * lane, 512)],
+            lambda gz, gx, gc: aligned(640 * gc + 160 * gz + 80 * gx, 80, 80), f_send.at[lane], f_recv.at[lane],
+        )
+        for lane in range(2)
+    ]
     onward = {1: (5, 6, 4), 2: (8, 7), 3: (9,), 5: (10,), 6: (12, 11), 8: (13,), 12: (14,)}
 
     def forward(gather, number):
@@ -144,7 +146,8 @@
 
     for number in onward:
         ops["A%d" % number] = functools.partial(forward, gather_a, number)
-        ops["F%d" % number] = functools.partial(forward, gather_f, number)
+        ops["F%d" % number] = functools.partial(forward, gather_out[0], number)
+        ops["H%d" % number] = functools.partial(forward, gather_out[1], number)
     ops["Ax"] = functools.partial(gather_a.start, 1)
 
     def g_slot(gy, gx):
@@ -194,70 +197,93 @@
     def e_rows(ez):
         return aligned(160 * ez, 160, 160)
 
-    left, right = pl.ds(0, 512), pl.ds(512, 512)
-    e = [
-        remote(part_out.at[e_rows(z2), left], land_z.at[0], e_send, e_recv, 0, to_zp),
-        remote(part_out.at[e_rows(z2), right], land_z.at[1], e_send, e_recv, 1, to_zm),
-        remote(part_out.at[e_rows(zm), left], land_z.at[2], e_send, e_recv, 2, to_zm),
-        remote(part_out.at[e_rows(zp), right], land_z.at[3], e_send, e_recv, 3, to_zp),
-        remote(part_out.at[e_rows(zp), left], land_z.at[4], e_send, e_recv, 4, to_zp),
-        remote(part_out.at[e_rows(zm), right], land_z.at[5], e_send, e_recv, 5, to_zm),
-        remote(part_out.at[aligned(160 * z + 80 * (1 - xhi), 80, 80)], land_h, e_send, e_recv, 6, to_xhi),
-    ]
-
-    def out_matmul():
-        loads["basis_out"].wait()
-        d[8].wait_recv()
-        d[9].wait_recv()
-
-        @pl.loop(0, 4)
-        def _(n):
-            rows = aligned(160 * n, 160, 160)
-            part_out[rows, :] = jnp.dot(
-                g_buf[aligned(640 * core + 160 * n, 160, 160), :], bo_buf[...], preferred_element_type=F32
-            ) + jnp.dot(g_twin[rows, :], bo_twin[...], preferred_element_type=F32)
-
-        for copy in e[:4]:
-            copy.start()
-
-    def out_a():
-        e[0].wait_recv()
-        part_out[e_rows(zp), left] += land_z[0]
-        e[4].start()
-
-    def out_b():
-        e[1].wait_recv()
-        part_out[e_rows(zm), right] += land_z[1]
-        e[5].start()
-
-    def out_sum():
-        for copy in e[2:6]:
-            copy.wait_recv()
-        part_out[e_rows(z), left] += land_z[4] + land_z[2]
-        part_out[e_rows(z), right] += land_z[5] + land_z[3]
-        e[6].start()
-
-    def out_final():
-        e[6].wait_recv()
-        rot_out[aligned(640 * core + 160 * z + 80 * xhi, 80, 80), :] = (
-            part_out[aligned(160 * z + 80 * xhi, 80, 80), :] + land_h[...]
-        ).astype(BF16)
-        gather_f.start(1, 2, 3, 0)
+    class Lane:
+        def __init__(self, lane):
+            self.lane, self.cols = lane, pl.ds(512 * lane, 512)
+            self.left, self.right = pl.ds(512 * lane, 256), pl.ds(512 * lane + 256, 256)
+
+            def term(number, ez, cols, device):
+                return remote(
+                    part_out.at[e_rows(ez), cols], land_z.at[lane, number], e_send.at[lane], e_recv.at[lane], number, device
+                )
+
+            self.e = [
+                term(0, z2, self.left, to_zp),
+                term(1, z2, self.right, to_zm),
+                term(2, zm, self.left, to_zm),
+                term(3, zp, self.right, to_zp),
+                term(4, zp, self.left, to_zp),
+                term(5, zm, self.right, to_zm),
+                remote(
+                    part_out.at[aligned(160 * z + 80 * (1 - xhi), 80, 80), self.cols],
+                    land_h.at[lane], e_send.at[lane], e_recv.at[lane], 6, to_xhi,
+                ),
+            ]
+
+        def matmul(self):
+            if self.lane == 0:
+                loads["basis_out"].wait()
+                d[8].wait_recv()
+                d[9].wait_recv()
+
+            @pl.loop(0, 2)
+            def _(n):
+                rows = aligned(320 * n, 320, 320)
+                part_out[rows, self.cols] = jnp.dot(
+                    g_buf[aligned(640 * core + 320 * n, 320, 320), :], bo_buf[:, self.cols], preferred_element_type=F32
+                ) + jnp.dot(g_twin[rows, :], bo_twin[:, self.cols], preferred_element_type=F32)
+
+            for copy in self.e[:4]:
+                copy.start()
+
+        def second_a(self):
+            self.e[0].wait_recv()
+            part_out[e_rows(zp), self.left] += land_z[self.lane, 0]
+            self.e[4].start()
+
+        def second_b(self):
+            self.e[1].wait_recv()
+            part_out[e_rows(zm), self.right] += land_z[self.lane, 1]
+            self.e[5].start()
+
+        def total(self):
+            for copy in self.e[2:6]:
+                copy.wait_recv()
+            part_out[e_rows(z), self.left] += land_z[self.lane, 4] + land_z[self.lane, 2]
+            part_out[e_rows(z), self.right] += land_z[self.lane, 5] + land_z[self.lane, 3]
+            self.e[6].start()
+
+        def finish(self):
+            self.e[6].wait_recv()
+            rot_out[aligned(640 * core + 160 * z + 80 * xhi, 80, 80), self.cols] = (
+                part_out[aligned(160 * z + 80 * xhi, 80, 80), self.cols] + land_h[self.lane]
+            ).astype(BF16)
+            gather_out[self.lane].start(1, 2, 3, 0)
+
+    lanes = [Lane(0), Lane(1)]
+    for lane in lanes:
+        ops["outmm%d" % lane.lane] = lane.matmul
+        ops["outa%d" % lane.lane] = lane.second_a
+        ops["outb%d" % lane.lane] = lane.second_b
+        ops["outsum%d" % lane.lane] = lane.total
+        ops["outfin%d" % lane.lane] = lane.finish
 
     def out_done():
-        gather_f.wait(0, 4, 7, 9, 10, 11, 13, 14)
-
-    ops.update(outmm=out_matmul, outa=out_a, outb=out_b, outsum=out_sum, outfin=out_final, Fdone=out_done)
+        for gather in gather_out:
+            gather.wait(0, 4, 7, 9, 10, 11, 13, 14)
+
+    ops["Fdone"] = out_done
 
     class Unit:
         def __init__(self, u):
             self.u, self.slot = u, u % SLOTS
-            if u < 2:
-                self.start = 160 * (2 * z + (xhi, 1 - xhi)[u])
-                self.need = ((0,), (4,))[u]
+            if u < 6:
+                block_z, block_x = (z, z, zm, zp, zm, zp)[u], (xhi, 1 - xhi, xhi, xhi, 1 - xhi, 1 - xhi)[u]
+                self.start = 160 * (2 * block_z + block_x)
+                self.need = ((0,), (4,), (7,), (9,), (10,), (11,))[u]
             else:
-                self.start = 320 * (zm, zp, z2)[(u - 2) % 3]
-                self.need = ((7, 10), (9, 11), (13, 14))[(u - 2) % 3]
+                self.start = 320 * z2
+                self.need = (13, 14)
             big, small = pl.ds(0, 48), pl.ds(48, 32)
             self.h = (big, small)
             if u % 2 == 0:
@@ -285,7 +311,7 @@
                 term(5, self.down, small, 2, to_down),
                 remote(send.at[u, y], land.at[u, 3], u_send.at[u], u_recv.at[u], 6, to_xlo),
             ]
-            self.pieces = 2 if u >= 5 else 1
+            self.pieces = 2 if u == 7 else 1
             for piece in range(self.pieces):
                 number = 7 + 4 * piece
                 self.copies += [
@@ -296,25 +322,23 @@
                 ]
 
         def place(self, owner, offset=0, count=80, piece=None):
-            if self.u < 2:
+            if self.u < 6:
                 rows = aligned(self.start + 80 * (owner // 2) + offset, 16, count)
                 return rows, aligned(HALF * lax.rem(owner, 2), 128, HALF)
             rows = aligned(self.start + 80 * owner + offset, 16, count)
-            if self.u < 5:
+            if self.u == 6:
                 return rows, pl.ds(0, HALF)
             return rows, (pl.ds(HALF, HALF), pl.ds(HALF, 384), pl.ds(HALF + 384, 512))[0 if piece is None else 1 + piece]
 
         def matmul(self):
             if self.u == 0:
                 loads["act"].wait()
-                loads["basis_in"].wait()
             gather_a.wait(*[number for number in self.need if number not in arrived])
             arrived.update(self.need)
-            if self.u < 2:
+            if self.u < 6:
                 rows = aligned(self.start, 160, 160)
 
-                @pl.loop(0, 2)
-                def _(n):
+                def columns(n):
                     block = jnp.dot(
                         a_buf[rows, :], b_buf[:, aligned(HALF * n, HALF, HALF)], preferred_element_type=F32
                     )
@@ -322,10 +346,19 @@
                         piece = block[80 * half:80 * half + 80]
                         part[self.slot, 2 * half + n] = piece
                         send[self.u, 2 * half + n] = piece.astype(BF16)
+
+                if self.u == 0:
+                    loads["basis_in_0"].wait()
+                    columns(0)
+                    loads["basis_in_1"].wait()
+                    columns(1)
+                    loads["eigen"].start()
+                else:
+                    pl.loop(0, 2)(columns)
             else:
                 block = jnp.dot(
                     a_buf[aligned(self.start, 320, 320), :],
-                    b_buf[:, HALF * ((self.u - 2) // 3):HALF * ((self.u - 2) // 3) + HALF],
+                    b_buf[:, HALF * (self.u - 6):HALF * (self.u - 6) + HALF],
                     preferred_element_type=F32,
                 )
                 for owner in range(4):
@@ -437,6 +470,8 @@
     d[0].start()
     d[1].start()
     d[9].start()
+    for name in ("act", "basis_in_0", "basis_in_1", "grad", "basis_out"):
+        loads[name].start()
     for names in ORDER:
         for name in names:
             ops[name]()
@@ -463,8 +498,9 @@
     col_copies = everyone(red_col, col, col_mates, c_send, c_recv)
     scores[...] = jnp.sum(red_col[...], axis=0)[:PAIRS, :64]
 
-    gather_f.finish()
-    for copy in d + e + row_copies + col_copies:
+    for gather in gather_out:
+        gather.finish()
+    for copy in d + lanes[0].e + lanes[1].e + row_copies + col_copies:
         copy.wait_send()
     for unit in units:
         for copy in unit.copies:
@@ -492,8 +528,8 @@
             pltpu.VMEM((512, 1024), BF16),
             pltpu.VMEM((512, 1024), BF16),
             pltpu.VMEM((640, 1024), F32),
-            pltpu.VMEM((6, 160, 512), F32),
-            pltpu.VMEM((80, 1024), F32),
+            pltpu.VMEM((2, 6, 160, 256), F32),
+            pltpu.VMEM((2, 80, 512), F32),
             pltpu.VMEM((1280, 1024), BF16),
             pltpu.VMEM((1024, 1792), F32),
             pltpu.VMEM((8 * PAIRS, 256), F32),
@@ -501,12 +537,12 @@
             pltpu.VMEM((16, 8, 128), F32),
             dma((15,)), dma((15,)),
             dma((10,)), dma((10,)),
-            dma((7,)), dma((7,)),
-            dma((15,)), dma((15,)),
+            dma((2, 7)), dma((2, 7)),
+            dma((2, 15)), dma((2, 15)),
             dma((8, 15)), dma((8, 15)),
             dma((7,)), dma((7,)),
             dma((15,)), dma((15,)),
-            dma((5,)),
+            dma((6,)),
         ],
         compiler_params=pltpu.CompilerParams(
             collective_id=0, has_side_effects=True, vmem_limit_bytes=63 * 2**20

time: 134 us -> 129 us (0.963)
  Pallas kernels: 133 us -> 128 us
    pallas_call x1, Pallas kernels: 133 us -> 128 us  [on_device(): pl.pallas_call(kernel, out_shape=jax.ShapeDtypeStruct((PAIRS, 64), F32),...]
where the time goes in v4:
time: 129 us
  Pallas kernels  128 us (99%)
    pallas_call x1, Pallas kernels, on_device(): pl.pallas_call(kernel, out_shape=jax.ShapeDtypeStruct((PAIRS, 64), F32),...  128 us

profile of v4, /device:TPU:1, one launch (start us, length us, event | category | flops | bytes accessed | tf_op | source)
XLA Modules:
  0.0 129.3 jit_solution(13042852073315993448)
XLA Ops:
  0.0 128.0 %shard_map.64 = f32[4,64]{1,0:T(4,128)} custom-call(bf16[80,3584]{1,0:T(8,128)(2,1)} %act.1, bf16[160,512]{1,0:T(8,128)(2,1)} %grad.1, bf16[3584,1792]{1,0:T(8,128)(2,1)} %basis_in.1, bf16[512,1024]{1,0:T(8,128)(2,1)} %basis_out.1, f32[1024,1792]{1,0:T(8,128)} %eigen.1, s32[1,1024]{1,0:T(1,128)} %bitcast.1), custom_call_target="tpu_custom_call" | custom-call | flops 28000000000 | bytes 22000000 | tf_op jit(solution)/shard_map/pallas_call | solution.py:514
  128.0 1.3 copy.8

commit v5 on v4

--- a/solution.py
+++ b/solution.py
@@ -83,14 +83,14 @@
 
 
 ORDER = (
-    ("Ax", "mm0", "Dc2", "Da", "sb0", "Db", "sa0", "A1", "A3", "th0", "Dc7", "A2", "Dc6", "mm1", "fo0", "mm3"),
-    ("mm2", "Dc4", "A6", "sb1", "fa0", "sa1", "A5", "fb0", "mm5", "Dx", "sa3", "sb3", "sb2", "mm4", "outmm0"),
-    ("la0", "sa2", "th1", "sa4", "sa5", "th3", "outmm1", "rcp", "A8", "sb5", "outa0", "A12", "th2", "fo1", "sb4"),
-    ("fo3", "th5", "mm6", "outb0", "fo2", "outb1", "th4", "fa1", "mm7", "sa6", "outa1", "sb6", "outsum0", "fb2"),
-    ("outsum1", "sb7", "outfin0", "fb1", "fa3", "fo5", "th6", "outfin1", "sa7", "fo4", "H2", "F3", "F1", "la1"),
-    ("H1", "fo6", "H8", "fb5", "H3", "fa5", "th7", "fa2", "fb3", "F2", "H6", "fb6", "F6", "fo7", "fa6", "H12"),
-    ("la3", "F8", "F5", "la5", "H5", "fb4", "la2", "F12", "fa4", "go7", "fa7", "fb7", "la6", "Fdone", "prep"),
-    ("la4", "fin0", "gb7", "la7", "ga7", "fin1", "ka7", "fin2"),
+    ("Ax", "mm0", "Da", "Dc2", "sa0", "sb0", "A3", "A1", "th0", "Dc4", "Db", "mm3", "fo0", "A2", "mm1", "Dc7"),
+    ("mm2", "A5", "sb3", "A6", "sa3", "Dc6", "sa1", "rcp", "sb1", "mm4", "sa2", "Dx", "sb2", "mm5", "outmm0"),
+    ("sb4", "A8", "th1", "A12", "sa4", "sb5", "sa5", "th3", "th2", "outb0", "fo1", "outa0", "mm6", "th5", "fo3"),
+    ("outmm1", "fo2", "fb0", "outsum0", "sb6", "fa0", "outb1", "sa6", "th4", "outa1", "mm7", "outfin0", "fb2"),
+    ("fo4", "fb1", "fa2", "fa1", "fb3", "outsum1", "sb7", "th6", "F1", "fa3", "F3", "sa7", "F6", "la0", "outfin1"),
+    ("fa4", "fb4", "F2", "fo5", "la1", "fo6", "go5", "H1", "F12", "th7", "H2", "H6", "H5", "fo7", "la3", "H3"),
+    ("fa6", "fb6", "la2", "F8", "fb5", "H12", "F5", "go7", "H8", "Fdone", "fa5", "gb5", "la4", "prep", "ga5"),
+    ("fb7", "fa7", "la6", "fin0", "ga7", "la5", "la7", "gb7", "ka5", "fin1", "ka7", "fin2"),
 )
 
 
@@ -122,9 +122,10 @@
         "eigen": pltpu.make_async_copy(eigen, eig, local.at[4]),
     }
     barrier = pltpu.get_barrier_semaphore()
-    for mate in row_mates + col_mates:
-        pl.semaphore_signal(barrier, inc=1, device_id=mate, device_id_type=MESH)
-    pl.semaphore_wait(barrier, len(row_mates) + len(col_mates))
+    friends = (to_yp, to_ym, to_zp, to_zm, to_xlo, to_xhi, to_core)
+    for friend in friends:
+        pl.semaphore_signal(barrier, inc=1, device_id=friend, device_id_type=MESH)
+    pl.semaphore_wait(barrier, len(friends))
 
     ops = {}
 
@@ -277,13 +278,17 @@
     class Unit:
         def __init__(self, u):
             self.u, self.slot = u, u % SLOTS
-            if u < 6:
-                block_z, block_x = (z, z, zm, zp, zm, zp)[u], (xhi, 1 - xhi, xhi, xhi, 1 - xhi, 1 - xhi)[u]
+            if u < 4:
+                block_z, block_x = (z, z, zm, zp)[u], (xhi, 1 - xhi, xhi, xhi)[u]
                 self.start = 160 * (2 * block_z + block_x)
-                self.need = ((0,), (4,), (7,), (9,), (10,), (11,))[u]
+                self.need = ((0,), (4,), (7,), (9,))[u]
+            elif u < 6:
+                self.starts = 160 * (2 * zm + 1 - xhi), 160 * (2 * zp + 1 - xhi)
+                self.need = (10, 11)
             else:
                 self.start = 320 * z2
                 self.need = (13, 14)
+            self.half = u % 2
             big, small = pl.ds(0, 48), pl.ds(48, 32)
             self.h = (big, small)
             if u % 2 == 0:
@@ -311,7 +316,7 @@
                 term(5, self.down, small, 2, to_down),
                 remote(send.at[u, y], land.at[u, 3], u_send.at[u], u_recv.at[u], 6, to_xlo),
             ]
-            self.pieces = 2 if u == 7 else 1
+            self.pieces = 2 if u in (5, 7) else 1
             for piece in range(self.pieces):
                 number = 7 + 4 * piece
                 self.copies += [
@@ -322,11 +327,15 @@
                 ]
 
         def place(self, owner, offset=0, count=80, piece=None):
-            if self.u < 6:
+            if self.u < 4:
                 rows = aligned(self.start + 80 * (owner // 2) + offset, 16, count)
                 return rows, aligned(HALF * lax.rem(owner, 2), 128, HALF)
-            rows = aligned(self.start + 80 * owner + offset, 16, count)
-            if self.u == 6:
+            if self.u < 6:
+                start = self.starts[0] + (owner // 2) * (self.starts[1] - self.starts[0]) + 80 * lax.rem(owner, 2)
+            else:
+                start = self.start + 80 * owner
+            rows = aligned(start + offset, 16, count)
+            if self.half == 0:
                 return rows, pl.ds(0, HALF)
             return rows, (pl.ds(HALF, HALF), pl.ds(HALF, 384), pl.ds(HALF + 384, 512))[0 if piece is None else 1 + piece]
 
@@ -335,7 +344,7 @@
                 loads["act"].wait()
             gather_a.wait(*[number for number in self.need if number not in arrived])
             arrived.update(self.need)
-            if self.u < 6:
+            if self.u < 4:
                 rows = aligned(self.start, 160, 160)
 
                 def columns(n):
@@ -356,15 +365,16 @@
                 else:
                     pl.loop(0, 2)(columns)
             else:
-                block = jnp.dot(
-                    a_buf[aligned(self.start, 320, 320), :],
-                    b_buf[:, HALF * (self.u - 6):HALF * (self.u - 6) + HALF],
-                    preferred_element_type=F32,
-                )
-                for owner in range(4):
-                    piece = block[80 * owner:80 * owner + 80]
-                    part[self.slot, owner] = piece
-                    send[self.u, owner] = piece.astype(BF16)
+                cols = slice(HALF * self.half, HALF * self.half + HALF)
+                sets = [(start, 160) for start in self.starts] if self.u < 6 else [(self.start, 320)]
+                owner = 0
+                for start, count in sets:
+                    block = jnp.dot(a_buf[aligned(start, 160, count), :], b_buf[:, cols], preferred_element_type=F32)
+                    for first in range(0, count, 80):
+                        piece = block[first:first + 80]
+                        part[self.slot, owner] = piece
+                        send[self.u, owner] = piece.astype(BF16)
+                        owner += 1
             for copy in self.copies[:4]:
                 copy.start()
 
@@ -439,28 +449,25 @@
         acc[...] = jnp.zeros_like(acc)
 
     def final(chunks):
-        @pl.loop(0, 2)
-        def _(n):
-            rows = aligned(512 * n, 512, 512)
-            query = a_buf[rows, QUERY_AT:QUERY_AT + 256].astype(F32)
-            for chunk in chunks:
-                cols = slice(256 * chunk, 256 * chunk + 256)
-                inverse = eig[rows, cols]
-                scaled = []
-                for first, last, at in WINDOWS:
-                    pair_block = jnp.dot(
-                        a_buf[rows, at:at + last - first], rot_in[first:last, cols], preferred_element_type=F32
-                    )
-                    scaled.append((pair_block * inverse).astype(BF16))
-                mapped = lax.dot_general(
-                    jnp.concatenate(scaled, axis=0),
-                    rot_in[1024:1280, cols],
-                    (((1,), (1,)), ((), ())),
-                    preferred_element_type=F32,
+        query = a_buf[0:1024, QUERY_AT:QUERY_AT + 256].astype(F32)
+        for chunk in chunks:
+            cols = slice(256 * chunk, 256 * chunk + 256)
+            inverse = eig[:, cols]
+            scaled = []
+            for first, last, at in WINDOWS:
+                pair_block = jnp.dot(
+                    a_buf[0:1024, at:at + last - first], rot_in[first:last, cols], preferred_element_type=F32
                 )
-                for p in range(PAIRS):
-                    product = mapped[512 * p:512 * p + 512] * query
-                    acc[8 * p:8 * p + 8, :] += jnp.sum(product.reshape(64, 8, 256), axis=0)
+                scaled.append((pair_block * inverse).astype(BF16))
+            mapped = lax.dot_general(
+                jnp.concatenate(scaled, axis=0),
+                rot_in[1024:1280, cols],
+                (((1,), (1,)), ((), ())),
+                preferred_element_type=F32,
+            )
+            for p in range(PAIRS):
+                product = mapped[1024 * p:1024 * p + 1024] * query
+                acc[8 * p:8 * p + 8, :] += jnp.sum(product.reshape(128, 8, 256), axis=0)
 
     ops.update(rcp=reciprocal, prep=prepare)
     for number, chunks in enumerate(((0, 1, 2), (3, 4), (5, 6))):

time: 129 us -> 125 us (0.969)
  Pallas kernels: 128 us -> 124 us
    pallas_call x1, Pallas kernels: 128 us -> 124 us  [on_device(): pl.pallas_call(kernel, out_shape=jax.ShapeDtypeStruct((PAIRS, 64), F32),...]
where the time goes in v5:
time: 125 us
  Pallas kernels  124 us (99%)
  local copies, waits for them, and re-layouts  1.26 us (1%)
    pallas_call x1, Pallas kernels, on_device(): pl.pallas_call(kernel, out_shape=jax.ShapeDtypeStruct((PAIRS, 64), F32),...  124 us

profile of v5, /device:TPU:1, one launch (start us, length us, event | category | flops | bytes accessed | tf_op | source)
XLA Modules:
  0.0 124.9 jit_solution(8997979998946356915)
XLA Ops:
  0.0 123.6 %shard_map.64 = f32[4,64]{1,0:T(4,128)} custom-call(bf16[80,3584]{1,0:T(8,128)(2,1)} %act.1, bf16[160,512]{1,0:T(8,128)(2,1)} %grad.1, bf16[3584,1792]{1,0:T(8,128)(2,1)} %basis_in.1, bf16[512,1024]{1,0:T(8,128)(2,1)} %basis_out.1, f32[1024,1792]{1,0:T(8,128)} %eigen.1, s32[1,1024]{1,0:T(1,128)} %bitcast.1), custom_call_target="tpu_custom_call" | custom-call | flops 28000000000 | bytes 22000000 | tf_op jit(solution)/shard_map/pallas_call | solution.py:521
  123.6 1.3 %copy.8 = f32[4,64]{1,0:T(4,128)} copy(f32[4,64]{1,0:T(4,128)} %shard_map.64) | data formatting | bytes 2048

commit v6 on v5

--- a/solution.py
+++ b/solution.py
@@ -113,11 +113,13 @@
     row_mates = [(lax.rem(row + k, 8), col) for k in range(1, 8)]
     col_mates = [(row, lax.rem(col + k, 16)) for k in range(1, 16)]
 
+    parity = lax.rem(y, 2)
+    first_half, second_half = aligned(HALF * parity, HALF, HALF), aligned(HALF * (1 - parity), HALF, HALF)
     loads = {
         "act": pltpu.make_async_copy(act, a_buf.at[aligned(80 * (4 * z + 2 * xhi + core), 80, 80)], local.at[0]),
         "grad": pltpu.make_async_copy(grad, g_buf.at[aligned(160 * (4 * xlo + y), 160, 160)], local.at[1]),
-        "basis_in_0": pltpu.make_async_copy(basis_in.at[:, pl.ds(0, HALF)], b_buf.at[:, pl.ds(0, HALF)], local.at[2]),
-        "basis_in_1": pltpu.make_async_copy(basis_in.at[:, pl.ds(HALF, HALF)], b_buf.at[:, pl.ds(HALF, HALF)], local.at[5]),
+        "basis_in_0": pltpu.make_async_copy(basis_in.at[:, first_half], b_buf.at[:, first_half], local.at[2]),
+        "basis_in_1": pltpu.make_async_copy(basis_in.at[:, second_half], b_buf.at[:, second_half], local.at[5]),
         "basis_out": pltpu.make_async_copy(basis_out, bo_buf, local.at[3]),
         "eigen": pltpu.make_async_copy(eigen, eig, local.at[4]),
     }
@@ -358,9 +360,11 @@
 
                 if self.u == 0:
                     loads["basis_in_0"].wait()
-                    columns(0)
+                    columns(parity)
+                    self.copies[0].start()
+                    self.copies[1].start()
                     loads["basis_in_1"].wait()
-                    columns(1)
+                    columns(1 - parity)
                     loads["eigen"].start()
                 else:
                     pl.loop(0, 2)(columns)
@@ -375,7 +379,7 @@
                         part[self.slot, owner] = piece
                         send[self.u, owner] = piece.astype(BF16)
                         owner += 1
-            for copy in self.copies[:4]:
+            for copy in self.copies[2 if self.u == 0 else 0:4]:
                 copy.start()
 
         def second(self, number):

time: 125 us -> 125 us (level)
  no operation moved by 1% of the time
where the time goes in v6:
time: 125 us
  Pallas kernels  124 us (99%)
  local copies, waits for them, and re-layouts  1.26 us (1%)
    pallas_call x1, Pallas kernels, on_device(): pl.pallas_call(kernel, out_shape=jax.ShapeDtypeStruct((PAIRS, 64), F32),...  124 us

profile of v6, /device:TPU:1, one launch (start us, length us, event | category | flops | bytes accessed | tf_op | source)
XLA Modules:
  0.0 124.9 jit_solution(13266137872526394460)
XLA Ops:
  0.0 123.6 %shard_map.64 = f32[4,64]{1,0:T(4,128)} custom-call(bf16[80,3584]{1,0:T(8,128)(2,1)} %act.1, bf16[160,512]{1,0:T(8,128)(2,1)} %grad.1, bf16[3584,1792]{1,0:T(8,128)(2,1)} %basis_in.1, bf16[512,1024]{1,0:T(8,128)(2,1)} %basis_out.1, f32[1024,1792]{1,0:T(8,128)} %eigen.1, s32[1,1024]{1,0:T(1,128)} %bitcast.1), custom_call_target="tpu_custom_call" | custom-call | flops 28000000000 | bytes 22000000 | tf_op jit(solution)/shard_map/pallas_call | solution.py:525
  123.6 1.3 %copy.8 = f32[4,64]{1,0:T(4,128)} copy(f32[4,64]{1,0:T(4,128)} %shard_map.64) | data formatting | bytes 2048
